TPU v7x, 256 devices: a whole 4x4x8 slice. The times are simulated.
256 devices in a mesh: mem: 8 (over x, core), tile: 32 (over z, y).
Axes of the slice: x: 4, y: 4, z: 8, core: 2. Of those that a mesh axis runs over, the one named last changes fastest.
Arguments:
- prior_sample: bfloat16 [256, 8, 256, 256], P('mem', None, 'tile'), may hold values from -6 to 6
- measured_position: int32 [256, 2, 256], P(('mem', 'tile')), may hold values from 0 to 1023
- measured_tally: int32 [256, 2], P(('mem', 'tile')), may hold values from 1 to 256, as said below
- measured_datum: float32 [256, 2, 256], P(('mem', 'tile')), may hold values from -6 to 6
- measured_noise_spread: bfloat16 [256, 2, 256], P(('mem', 'tile')), may hold values from 0.25 to 4
Outputs:
- analysis: bfloat16 [256, 8, 256, 256], P('mem', None, 'tile')
Inputs may be any that keep to these rules, and one draw needn't show every extreme that they name: `measured_tally`: counts are uneven from row to row, and some block in every draw has all 256 slots live.
All inputs are finite; a program needn't handle non-finite values.
Results may differ from a plain program's by a relative error of at most 0.0055.
The roundings to bfloat16 on the way count: a program that leaves them out, or rounds other values in their place, can miss the bound.
Values may be sent and summed in bfloat16 or wider, within the bound.
No kernel may reach another device: no remote copies, remote signals or barrier semaphores. Data moves between devices by JAX's collectives and lax.ppermute only.
A program may use at most 64 MiB of HBM per device.

v0:
```python
import math

import jax
import jax.numpy as jnp
from jax import lax
from jax.experimental import pallas as pl
from jax.experimental.pallas import tpu as pltpu
from jax.sharding import PartitionSpec as P

TILE_WIDTH = 128
MEM = ("mem", "tile")
VMEM_LIMIT = 48 * 1024 * 1024
F32 = jnp.float32
BF16 = jnp.bfloat16
NT = (((1,), (1,)), ((), ()))
NN = (((1,), (0,)), ((), ()))


def dot(a, b, dims=NN):
    return lax.dot_general(a, b, dims, preferred_element_type=F32)


def dot_full(a, b, dims=NN):
    return lax.dot_general(
        a, b, dims, precision=lax.Precision.HIGHEST, preferred_element_type=F32
    )


def call(body, out_shape, in_specs=None, scratch=()):
    extra = {} if in_specs is None else {"in_specs": in_specs}
    return pl.pallas_call(
        body,
        out_shape=out_shape,
        scratch_shapes=scratch,
        compiler_params=pltpu.CompilerParams(vmem_limit_bytes=VMEM_LIMIT),
        **extra,
    )


def eye(rows, cols, shift=0):
    down = lax.broadcasted_iota(jnp.int32, (rows, cols), 0)
    along = lax.broadcasted_iota(jnp.int32, (rows, cols), 1)
    return jnp.where(along == down + shift, 1.0, 0.0).astype(F32)


def split_kernel(x_ref, out_ref, wide_ref):
    rows = x_ref.shape[1]
    unit = eye(rows, rows).astype(BF16)
    for g in range(16):
        both = jnp.concatenate(
            [x_ref[g * 64 : (g + 1) * 64, :], x_ref[(16 + g) * 64 : (17 + g) * 64, :]], axis=0
        )
        wide_ref[pl.ds(g, rows, stride=16), :] = dot(unit, both, NT)
    for r in range(0, rows, 32):
        out_ref[r : r + 32] = (
            wide_ref[r * 16 : (r + 32) * 16, :].astype(BF16).reshape(32, 16, 128)
        )


def merge_kernel(x_ref, out_ref, wide_ref):
    rows = x_ref.shape[0]
    for r in range(0, rows, 32):
        wide_ref[r * 16 : (r + 32) * 16, :] = x_ref[r : r + 32].reshape(32 * 16, 128).astype(F32)
    unit = eye(128, 128).astype(BF16)
    for g in range(16):
        part = wide_ref[pl.ds(g, rows, stride=16), :].astype(BF16)
        turned = dot(unit, part, NT).astype(BF16)
        out_ref[g * 64 : (g + 1) * 64, :] = turned[:64]
        out_ref[(16 + g) * 64 : (17 + g) * 64, :] = turned[64:]


def swap_halves(low, high):
    left = lax.broadcasted_iota(jnp.int32, low.shape, low.ndim - 1) < 64
    axis = low.ndim - 1
    first = jnp.where(left, low, pltpu.roll(high, 64, axis))
    second = jnp.where(left, pltpu.roll(low, 64, axis), high)
    return first, second


def observe_kernel(x_ref, pos_ref, datum_ref, noise_ref, tally_ref, anom_ref, avg_ref, pack_ref):
    members = anom_ref.shape[1]
    groups = x_ref.shape[0]
    for c in range(2):
        for tp in range(8):
            low = x_ref[:, c * 8 + tp, 0].astype(F32)
            high = x_ref[:, c * 8 + tp, 1].astype(F32)
            first, second = swap_halves(low, high)
            cells = jnp.concatenate([first, second], axis=1).reshape(groups * 32, 128)
            average = jnp.sum(cells, axis=0, keepdims=True) / members
            anom_ref[c, :, tp * 128 : (tp + 1) * 128] = (cells - average).astype(BF16)
            avg_ref[c, :, tp * 128 : (tp + 1) * 128] = average
        pos = pos_ref[c : c + 1, :]
        level, col = pos // 128, pos % 128
        place = (col // 8) * 64 + level * 8 + col % 8
        slots = pos.shape[1]
        cell_total = anom_ref.shape[2]
        chosen = lax.broadcasted_iota(jnp.int32, (cell_total, slots), 0) == place
        chosen = jnp.where(chosen, 1.0, 0.0).astype(BF16)
        pack_ref[c, :members, :] = dot(anom_ref[c], chosen).astype(BF16)
        average = avg_ref[c]
        top = average.astype(BF16)
        rest = average - top.astype(F32)
        middle = rest.astype(BF16)
        bottom = (rest - middle.astype(F32)).astype(BF16)
        pieces = jnp.concatenate(
            [top.astype(F32), middle.astype(F32), bottom.astype(F32)]
            + [jnp.zeros((13, cell_total), F32)],
            axis=0,
        ).astype(BF16)
        found = dot(pieces, chosen)
        found = found[0:1] + (found[1:2] + found[2:3])
        innovation = datum_ref[c : c + 1, :] - found
        live = lax.broadcasted_iota(jnp.int32, (1, slots), 1) < tally_ref[0, c]
        weights = jnp.where(live, 1.0 / noise_ref[c : c + 1, :].astype(F32), 0.0)
        sub = lax.broadcasted_iota(jnp.int32, (16, slots), 0)
        tail = jnp.where(sub == 0, innovation, jnp.where(sub == 1, weights, 0.0))
        pack_ref[c, members:, :] = tail.astype(BF16)


def invert64(rows):
    n = rows[0].shape[0]
    shape = (n, 8, 128)
    sub = lax.broadcasted_iota(jnp.int32, shape, 1)

    def lane(x, j):
        return jnp.broadcast_to(x[:, :, j : j + 1], shape)

    def sublane(x, i):
        return jnp.broadcast_to(x[:, i : i + 1, :], shape)

    rows = list(rows)
    for b in range(8):
        cols = {
            (i, j): lane(rows[i], 64 + 8 * b + j) for i in range(b, 8) for j in range(8)
        }
        pivots = None
        for r in range(8):
            pivot = sublane(cols[b, r], r)
            pivots = pivot if r == 0 else jnp.where(sub == r, pivot, pivots)
            inverse = 1.0 / pivot
            heads = {j: sublane(cols[b, j], r) for j in range(r + 1, 8)}
            factors = {}
            for i in range(b, 8):
                factor = cols[i, r] * inverse
                if i == b:
                    factor = jnp.where(sub > r, factor, 0.0)
                factors[i] = factor
            for i in range(b, 8):
                for j in range(r + 1, 8):
                    cols[i, j] = cols[i, j] - factors[i] * heads[j]
            row = sublane(rows[b], r)
            for i in range(b, 8):
                if i == b and r == 7:
                    continue
                rows[i] = rows[i] - factors[i] * row
        rows[b] = rows[b] * lax.rsqrt(pivots)
    return rows


def invert128(systems):
    n = len(systems)
    left = lax.broadcasted_iota(jnp.int32, (64, 128), 1) < 64
    unit_left = eye(64, 128)
    unit_right = eye(64, 128, 64)

    def run(blocks):
        stack = [
            jnp.stack([blk[8 * i : 8 * i + 8] for blk in blocks]) for i in range(8)
        ]
        done = invert64(stack)
        return [jnp.concatenate([done[i][m] for i in range(8)], axis=0) for m in range(n)]

    upper = [s[:64] for s in systems]
    first = run([jnp.where(left, unit_left, pltpu.roll(u, 64, 1)) for u in upper])
    tops = [jnp.where(left, f, 0.0) for f in first]
    firsts = [f[:, :64] for f in first]
    across = [dot_full(f, u) for f, u in zip(firsts, upper)]
    down = [dot_full(s[64:, :64], f, NT) for s, f in zip(systems, firsts)]
    lower = [s[64:] - dot_full(d, a) for s, d, a in zip(systems, down, across)]
    second = run([jnp.where(left, unit_left, low) for low in lower])
    joined = [
        jnp.where(left, -dot_full(d, t), unit_right) for d, t in zip(down, tops)
    ]
    bottoms = [dot_full(s[:, :64], j) for s, j in zip(second, joined)]
    return [jnp.concatenate([t, b], axis=0) for t, b in zip(tops, bottoms)]


def update_kernel(own_ref, up_ref, down_ref, anom_ref, avg_ref, out_ref):
    members = anom_ref.shape[1]
    groups = members // 32
    grams, forces = [], []
    for c in range(2):
        ens, wtd, inn = [], [], []
        for ref, falloff in ((own_ref, 1.0), (up_ref, 0.5), (down_ref, 0.5)):
            ensemble = ref[c, :members, :]
            tail = ref[c, members:, :]
            weights = tail[1:2, :].astype(F32)
            weighted = (weights * ensemble.astype(F32)).astype(BF16)
            ens.append(ensemble)
            wtd.append((weighted.astype(F32) * falloff).astype(BF16))
            inn.append(tail)
        ens = jnp.concatenate(ens, axis=1)
        wtd = jnp.concatenate(wtd, axis=1)
        inn = jnp.concatenate(inn, axis=1)
        grams.append(0.5 * (dot(wtd, ens, NT) + dot(ens, wtd, NT)))
        forces.append(dot(inn, wtd, NT)[0:1])
    spread = (members - 1) * eye(members, members)
    systems = [spread + (grams[c] + 0.5 * grams[1 - c]) for c in range(2)]
    forces = [forces[c] + 0.5 * forces[1 - c] for c in range(2)]
    tops = invert128([s[:128, :128] for s in systems])
    across = [dot_full(t, s[:128, 128:]) for t, s in zip(tops, systems)]
    down = [dot_full(s[128:, :128], t, NT) for t, s in zip(tops, systems)]
    lower = [s[128:, 128:] - dot_full(d, a) for s, d, a in zip(systems, down, across)]
    lows = invert128(lower)
    mixed = [dot_full(d, t) for d, t in zip(down, tops)]
    corners = [-dot_full(low, m) for low, m in zip(lows, mixed)]
    for c in range(2):
        top = jnp.concatenate([tops[c], jnp.zeros((128, 128), F32)], axis=1)
        bottom = jnp.concatenate([corners[c], lows[c]], axis=1)
        inverse = jnp.concatenate([top, bottom], axis=0)
        halfway = jnp.sum(inverse * forces[c], axis=1, keepdims=True)
        mean_weight = jnp.sum(inverse * halfway, axis=0, keepdims=True)
        mixing = (math.sqrt(members - 1) * inverse + mean_weight).astype(BF16)
        for tp in range(8):
            span = slice(tp * 128, (tp + 1) * 128)
            made = dot(mixing, anom_ref[c, :, span]) + avg_ref[c, :, span]
            made = made.reshape(groups, 32, 128)
            low, high = swap_halves(made[:, :16], made[:, 16:])
            out_ref[:, c * 8 + tp, 0] = low.astype(BF16)
            out_ref[:, c * 8 + tp, 1] = high.astype(BF16)


def on_device(
    prior_sample, measured_position, measured_tally, measured_datum, measured_noise_spread
):
    part, level_count, width, line_total = prior_sample.shape
    groups, tiles = lax.axis_size("mem"), lax.axis_size("tile")
    members = groups * part
    cells = level_count * TILE_WIDTH
    slots = measured_position.shape[2]
    chunk = (line_total, 16, 128)
    wide = [pltpu.VMEM((line_total * 16, 128), F32)]

    parted = call(split_kernel, jax.ShapeDtypeStruct(chunk, BF16), scratch=wide)(
        prior_sample.reshape(part * level_count * width, line_total)
    )
    relaid = lax.all_to_all(parted, MEM, split_axis=0, concat_axis=0, tiled=True)

    vmem = pl.BlockSpec(memory_space=pltpu.VMEM)
    anomaly, average, packed = call(
        observe_kernel,
        (
            jax.ShapeDtypeStruct((2, members, cells), BF16),
            jax.ShapeDtypeStruct((2, 1, cells), F32),
            jax.ShapeDtypeStruct((2, members + 16, slots), BF16),
        ),
        in_specs=[vmem, vmem, vmem, vmem, pl.BlockSpec(memory_space=pltpu.SMEM)],
    )(
        relaid.reshape(groups, tiles // 2, 2, 16, 128),
        measured_position[0],
        measured_datum[0],
        measured_noise_spread[0],
        measured_tally,
    )
    ends = line_total - 1
    above = lax.ppermute(packed, MEM, [(i, i + 1) for i in range(ends)])
    below = lax.ppermute(packed, MEM, [(i + 1, i) for i in range(ends)])
    analyzed = call(
        update_kernel,
        jax.ShapeDtypeStruct((groups, tiles // 2, 2, 16, 128), BF16),
    )(packed, above, below, anomaly, average)
    returned = lax.all_to_all(
        analyzed.reshape(chunk), MEM, split_axis=0, concat_axis=0, tiled=True
    )
    merged = call(
        merge_kernel,
        jax.ShapeDtypeStruct((part * level_count * width, line_total), BF16),
        scratch=wide,
    )(returned)
    return merged.reshape(part, level_count, width, line_total)


def solution(mesh):
    placed = (
        P("mem", None, "tile", None),
        P(MEM, None, None),
        P(MEM, None),
        P(MEM, None, None),
        P(MEM, None, None),
    )
    return jax.shard_map(
        on_device,
        mesh=mesh,
        in_specs=placed,
        out_specs=P("mem", None, "tile", None),
        check_vma=False,
    )
```

profile of v0, /device:TPU:1, one launch (start us, length us, event | category | flops | bytes accessed | tf_op | source)
XLA Modules:
  0.0 120.2 jit_solution(11506371195745326416)
XLA Ops:
  0.0 0.0 copy-start
  0.0 1.2 %copy-done = bf16[32,8,8,256]{3,2,1,0:T(8,128)(2,1)S(1)} copy-done((bf16[32,8,8,256]{3,2,1,0:T(8,128)(2,1)S(1)}, bf16[32,8,8,256]{3,2,1,0:T(8,128)(2,1)}, u32[]{:S(2)}) %copy-start) | copy-done | bytes 1048600
  1.2 1.0 shard_map.55
  2.2 46.6 %all_to_all.10 = bf16[256,16,128]{2,1,0:T(8,128)(2,1)S(1)} all-to-all(bf16[256,16,128]{2,1,0:T(8,128)(2,1)S(1)} %shard_map.55), channel_id=1, replica_groups=mesh['mem'=8,'tile'=32] {'mem','tile'}, dimensions={0} | all-to-all | bytes 2097152 | tf_op jit(solution)/shard_map/all_to_all | solution.py:247
  48.9 0.0 copy-start.2
  48.9 0.0 copy-start.1
  48.9 0.0 copy-start.3
  48.9 0.0 copy-start.4
  48.9 0.7 copy-done.2
  49.6 0.0 copy-done.1
  49.6 0.0 copy-done.3
  49.6 0.0 copy-done.4
  49.6 1.9 %shard_map.56 = (bf16[2,256,1024]{2,1,0:T(8,128)(2,1)S(1)}, f32[2,1,1024]{2,1,0:T(1,128)S(1)}, bf16[2,272,256]{2,1,0:T(8,128)(2,1)S(1)}) custom-call(bf16[8,16,2,16,128]{4,3,2,1,0:T(8,128)(2,1)S(1)} %bitcast.8, s32[2,256]{1,0:T(2,128)S(1)} %bitcast.10, f32[2,256]{1,0:T(2,128)S(1)} %bitcast.11, bf16[2,256]{1,0:T(2,128)(2,1)S(1)} %bitcast.12, s32[1,2]{1,0:T(1,128)S(1)} %copy-done.4), custom_call_target="tpu_custom_call" | custom-call | tf_op jit(solution)/shard_map/pallas_call | solution.py:250
  51.5 3.8 %collective-permute-start.1 = (bf16[2,272,256]{2,1,0:T(8,128)(2,1)S(1)}, bf16[2,272,256]{2,1,0:T(8,128)(2,1)S(1)}, u32[]{:S(2)}, u32[]{:S(2)}) collective-permute-start(bf16[2,272,256]{2,1,0:T(8,128)(2,1)S(1)} %get-tuple-element.8.own_ref), channel_id=1, source_target_pairs={{1,0},{2,1},{3,2},{4,3},{5,4},{6,5},{7,6},{8,7},{9,8},{10,9},{11,1... | collective-permute-start | bytes 835592 | tf_op jit(solution)/shard_map/ppermute | solution.py:267
  55.2 2.1 %collective-permute-start = (bf16[2,272,256]{2,1,0:T(8,128)(2,1)S(1)}, bf16[2,272,256]{2,1,0:T(8,128)(2,1)S(1)}, u32[]{:S(2)}, u32[]{:S(2)}) collective-permute-start(bf16[2,272,256]{2,1,0:T(8,128)(2,1)S(1)} %get-tuple-element.8.own_ref), channel_id=1, source_target_pairs={{0,1},{1,2},{2,3},{3,4},{4,5},{5,6},{6,7},{7,8},{8,9},{9,10},{10,1... | collective-permute-start | bytes 835592 | tf_op jit(solution)/shard_map/ppermute | solution.py:266
  57.3 4.3 %collective-permute-done.1.down_ref = bf16[2,272,256]{2,1,0:T(8,128)(2,1)S(1)} collective-permute-done((bf16[2,272,256]{2,1,0:T(8,128)(2,1)S(1)}, bf16[2,272,256]{2,1,0:T(8,128)(2,1)S(1)}, u32[]{:S(2)}, u32[]{:S(2)}) %collective-permute-start.1) | collective-permute-done | bytes 278560 | tf_op jit(solution)/shard_map/ppermute | solution.py:267
  61.6 7.6 %collective-permute-done.up_ref = bf16[2,272,256]{2,1,0:T(8,128)(2,1)S(1)} collective-permute-done((bf16[2,272,256]{2,1,0:T(8,128)(2,1)S(1)}, bf16[2,272,256]{2,1,0:T(8,128)(2,1)S(1)}, u32[]{:S(2)}, u32[]{:S(2)}) %collective-permute-start) | collective-permute-done | bytes 278560 | tf_op jit(solution)/shard_map/ppermute | solution.py:266
  69.2 12.7 %shard_map.57 = bf16[8,16,2,16,128]{4,3,2,1,0:T(8,128)(2,1)S(1)} custom-call(bf16[2,272,256]{2,1,0:T(8,128)(2,1)S(1)} %get-tuple-element.8.own_ref, bf16[2,272,256]{2,1,0:T(8,128)(2,1)S(1)} %collective-permute-done.up_ref, bf16[2,272,256]{2,1,0:T(8,128)(2,1)S(1)} %collective-permute-done.1.down_ref, bf16[2,256,1024]{2,1,0:T(8,128)(2,1)S(1)} %get-tuple-element.9.anom_ref, ...), custom_call_target="tpu_custom_call" | custom-call | tf_op jit(solution)/shard_map/pallas_call | solution.py:268
  81.9 36.3 %all_to_all.11.x_ref = bf16[256,16,128]{2,1,0:T(8,128)(2,1)S(1)} all-to-all(bf16[256,16,128]{2,1,0:T(8,128)(2,1)S(1)} %bitcast.7), channel_id=1, replica_groups=mesh['mem'=8,'tile'=32] {'mem','tile'}, dimensions={0} | all-to-all | bytes 2097152 | tf_op jit(solution)/shard_map/all_to_all | solution.py:272
  118.3 2.0 %shard_map.58 = bf16[2048,256]{1,0:T(8,128)(2,1)} custom-call(bf16[256,16,128]{2,1,0:T(8,128)(2,1)S(1)} %all_to_all.11.x_ref), custom_call_target="tpu_custom_call" | custom-call | tf_op jit(solution)/shard_map/pallas_call | solution.py:275
Async XLA Ops:
  0.0 1.2 %copy-start = (bf16[32,8,8,256]{3,2,1,0:T(8,128)(2,1)S(1)}, bf16[32,8,8,256]{3,2,1,0:T(8,128)(2,1)}, u32[]{:S(2)}) copy-start(bf16[32,8,8,256]{3,2,1,0:T(8,128)(2,1)} %param.5) | copy-start | bytes 3145732
  48.9 0.7 copy-start.2
  48.9 0.7 copy-start.1
  48.9 0.7 copy-start.3
  48.9 0.7 copy-start.4
  51.5 10.1 %collective-permute-start.1 = (bf16[2,272,256]{2,1,0:T(8,128)(2,1)S(1)}, bf16[2,272,256]{2,1,0:T(8,128)(2,1)S(1)}, u32[]{:S(2)}, u32[]{:S(2)}) collective-permute-start(bf16[2,272,256]{2,1,0:T(8,128)(2,1)S(1)} %get-tuple-element.8.own_ref), channel_id=1, source_target_pairs={{1,0},{2,1},{3,2},{4,3},{5,4},{6,5},{7,6},{8,7},{9,8},{10,9},{11,1... | collective-permute-start | bytes 835592 | tf_op jit(solution)/shard_map/ppermute | solution.py:267
  55.2 14.0 %collective-permute-start = (bf16[2,272,256]{2,1,0:T(8,128)(2,1)S(1)}, bf16[2,272,256]{2,1,0:T(8,128)(2,1)S(1)}, u32[]{:S(2)}, u32[]{:S(2)}) collective-permute-start(bf16[2,272,256]{2,1,0:T(8,128)(2,1)S(1)} %get-tuple-element.8.own_ref), channel_id=1, source_target_pairs={{0,1},{1,2},{2,3},{3,4},{4,5},{5,6},{6,7},{7,8},{8,9},{9,10},{10,1... | collective-permute-start | bytes 835592 | tf_op jit(solution)/shard_map/ppermute | solution.py:266
where the time goes:
time: 120 us
  blocking collectives  83 us (69%)
  Pallas kernels  17.6 us (15%)
  waiting for transfers between devices  11.9 us (10%)
  starting transfers between devices  5.85 us (5%)
  local copies, waits for them, and re-layouts  1.93 us (2%)
    all_to_all x1, blocking collectives, on_device(): lax.all_to_all(parted, MEM, split_axis=0, concat_axis=0, tiled=True)  46.6 us
    all_to_all x1, blocking collectives, on_device(): lax.all_to_all(analyzed.reshape(chunk), MEM, split_axis=0, concat_axis=0,...  36.3 us
    pallas_call x1, Pallas kernels, on_device(): call(update_kernel, jax.ShapeDtypeStruct((groups, tiles // 2, 2, 16, 128)...  12.7 us
    ppermute x1, waiting for transfers between devices, on_device(): above = lax.ppermute(packed, MEM, [(i, i + 1) for i in range(ends)])  7.6 us
    ppermute x1, waiting for transfers between devices, on_device(): below = lax.ppermute(packed, MEM, [(i + 1, i) for i in range(ends)])  4.27 us
    ppermute x1, starting transfers between devices, on_device(): below = lax.ppermute(packed, MEM, [(i + 1, i) for i in range(ends)])  3.75 us
  transfers between devices with their start and end apart: 2, of which 2 were waited for; matrix products, arithmetic and copies ran while one was open for 0% of the time, Pallas kernels for 0%

commit v1 on v0

--- a/solution.py
+++ b/solution.py
@@ -2,6 +2,7 @@
 
 import jax
 import jax.numpy as jnp
+import numpy as np
 from jax import lax
 from jax.experimental import pallas as pl
 from jax.experimental.pallas import tpu as pltpu
@@ -26,12 +27,15 @@
     )
 
 
-def call(body, out_shape, in_specs=None, scratch=()):
+def call(body, out_shape, in_specs=None, out_specs=None, scratch=(), cost=None):
     extra = {} if in_specs is None else {"in_specs": in_specs}
+    if out_specs is not None:
+        extra["out_specs"] = out_specs
     return pl.pallas_call(
         body,
         out_shape=out_shape,
         scratch_shapes=scratch,
+        cost_estimate=cost,
         compiler_params=pltpu.CompilerParams(vmem_limit_bytes=VMEM_LIMIT),
         **extra,
     )
@@ -43,30 +47,79 @@
     return jnp.where(along == down + shift, 1.0, 0.0).astype(F32)
 
 
-def split_kernel(x_ref, out_ref, wide_ref):
-    rows = x_ref.shape[1]
-    unit = eye(rows, rows).astype(BF16)
-    for g in range(16):
-        both = jnp.concatenate(
-            [x_ref[g * 64 : (g + 1) * 64, :], x_ref[(16 + g) * 64 : (17 + g) * 64, :]], axis=0
+def row_of(device):
+    x, core, z, y = device // 64, device // 32 % 2, device // 4 % 8, device % 4
+    along_y = y + (x % 2) * (3 - 2 * y)
+    along_z = z + (along_y % 2) * (7 - 2 * z)
+    return 2 * (x * 32 + along_y * 8 + along_z) + core
+
+
+def row_choice(total):
+    device = lax.broadcasted_iota(jnp.int32, (total, total), 0)
+    row = lax.broadcasted_iota(jnp.int32, (total, total), 1)
+    return jnp.where(row == row_of(device), 1.0, 0.0).astype(BF16)
+
+
+PIECES = 4
+
+
+def split_kernel(
+    x_ref, pos_ref, datum_ref, noise_ref, tally_ref, out_ref, obs_ref, held_ref, wide_ref, sems
+):
+    rows = x_ref.shape[2]
+    span = x_ref.shape[1] // PIECES
+    copies = [
+        pltpu.make_async_copy(
+            x_ref.at[:, pl.ds(i * span, span), :], held_ref.at[i], sems.at[i]
         )
-        wide_ref[pl.ds(g, rows, stride=16), :] = dot(unit, both, NT)
+        for i in range(PIECES)
+    ]
+    for copy in copies:
+        copy.start()
+    choice = row_choice(rows)
+    slots = pos_ref.shape[1]
+    pos = pos_ref[...]
+    level, col = pos // 128, pos % 128
+    obs_ref[0:2, :] = ((col // 8) * 64 + level * 8 + col % 8).astype(F32)
+    obs_ref[2:4, :] = datum_ref[...]
+    slot = lax.broadcasted_iota(jnp.int32, (1, slots), 1)
+    for c in range(2):
+        weights = 1.0 / noise_ref[c : c + 1, :].astype(F32)
+        obs_ref[4 + c : 5 + c, :] = jnp.where(slot < tally_ref[0, c], weights, 0.0)
+    obs_ref[6:8, :] = jnp.zeros((2, slots), F32)
+    for i in range(PIECES):
+        copies[i].wait()
+        for h in range(span // 64):
+            both = held_ref[i, :, h * 64 : (h + 1) * 64, :].reshape(128, rows)
+            g = i * (span // 64) + h
+            wide_ref[pl.ds(g, rows, stride=16), :] = dot(choice, both, NT)
     for r in range(0, rows, 32):
         out_ref[r : r + 32] = (
             wide_ref[r * 16 : (r + 32) * 16, :].astype(BF16).reshape(32, 16, 128)
         )
 
 
-def merge_kernel(x_ref, out_ref, wide_ref):
+def merge_kernel(x_ref, out_ref, held_ref, wide_ref, sems):
     rows = x_ref.shape[0]
+    span = out_ref.shape[1] // PIECES
     for r in range(0, rows, 32):
         wide_ref[r * 16 : (r + 32) * 16, :] = x_ref[r : r + 32].reshape(32 * 16, 128).astype(F32)
+    choice = row_choice(rows)
     unit = eye(128, 128).astype(BF16)
-    for g in range(16):
-        part = wide_ref[pl.ds(g, rows, stride=16), :].astype(BF16)
-        turned = dot(unit, part, NT).astype(BF16)
-        out_ref[g * 64 : (g + 1) * 64, :] = turned[:64]
-        out_ref[(16 + g) * 64 : (17 + g) * 64, :] = turned[64:]
+    copies = []
+    for i in range(PIECES):
+        for h in range(span // 64):
+            g = i * (span // 64) + h
+            part = wide_ref[pl.ds(g, rows, stride=16), :].astype(BF16)
+            turned = dot(dot(unit, part, NT).astype(BF16), choice).astype(BF16)
+            held_ref[i, :, h * 64 : (h + 1) * 64, :] = turned.reshape(2, 64, rows)
+        copy = pltpu.make_async_copy(
+            held_ref.at[i], out_ref.at[:, pl.ds(i * span, span), :], sems.at[i]
+        )
+        copy.start()
+        copies.append(copy)
+    for copy in copies:
+        copy.wait()
 
 
 def swap_halves(low, high):
@@ -77,9 +130,11 @@
     return first, second
 
 
-def observe_kernel(x_ref, pos_ref, datum_ref, noise_ref, tally_ref, anom_ref, avg_ref, pack_ref):
+def observe_kernel(x_ref, obs_ref, anom_ref, avg_ref, pack_ref):
     members = anom_ref.shape[1]
     groups = x_ref.shape[0]
+    cell_total = anom_ref.shape[2]
+    slots = pack_ref.shape[2]
     for c in range(2):
         for tp in range(8):
             low = x_ref[:, c * 8 + tp, 0].astype(F32)
@@ -89,11 +144,7 @@
             average = jnp.sum(cells, axis=0, keepdims=True) / members
             anom_ref[c, :, tp * 128 : (tp + 1) * 128] = (cells - average).astype(BF16)
             avg_ref[c, :, tp * 128 : (tp + 1) * 128] = average
-        pos = pos_ref[c : c + 1, :]
-        level, col = pos // 128, pos % 128
-        place = (col // 8) * 64 + level * 8 + col % 8
-        slots = pos.shape[1]
-        cell_total = anom_ref.shape[2]
+        place = obs_ref[c : c + 1, :].astype(jnp.int32)
         chosen = lax.broadcasted_iota(jnp.int32, (cell_total, slots), 0) == place
         chosen = jnp.where(chosen, 1.0, 0.0).astype(BF16)
         pack_ref[c, :members, :] = dot(anom_ref[c], chosen).astype(BF16)
@@ -109,9 +160,8 @@
         ).astype(BF16)
         found = dot(pieces, chosen)
         found = found[0:1] + (found[1:2] + found[2:3])
-        innovation = datum_ref[c : c + 1, :] - found
-        live = lax.broadcasted_iota(jnp.int32, (1, slots), 1) < tally_ref[0, c]
-        weights = jnp.where(live, 1.0 / noise_ref[c : c + 1, :].astype(F32), 0.0)
+        innovation = obs_ref[2 + c : 3 + c, :] - found
+        weights = obs_ref[4 + c : 5 + c, :]
         sub = lax.broadcasted_iota(jnp.int32, (16, slots), 0)
         tail = jnp.where(sub == 0, innovation, jnp.where(sub == 1, weights, 0.0))
         pack_ref[c, members:, :] = tail.astype(BF16)
@@ -185,13 +235,11 @@
     return [jnp.concatenate([t, b], axis=0) for t, b in zip(tops, bottoms)]
 
 
-def update_kernel(own_ref, up_ref, down_ref, anom_ref, avg_ref, out_ref):
-    members = anom_ref.shape[1]
-    groups = members // 32
+def tapered(sources, members):
     grams, forces = [], []
     for c in range(2):
         ens, wtd, inn = [], [], []
-        for ref, falloff in ((own_ref, 1.0), (up_ref, 0.5), (down_ref, 0.5)):
+        for ref, falloff in sources:
             ensemble = ref[c, :members, :]
             tail = ref[c, members:, :]
             weights = tail[1:2, :].astype(F32)
@@ -199,14 +247,32 @@
             ens.append(ensemble)
             wtd.append((weighted.astype(F32) * falloff).astype(BF16))
             inn.append(tail)
-        ens = jnp.concatenate(ens, axis=1)
-        wtd = jnp.concatenate(wtd, axis=1)
-        inn = jnp.concatenate(inn, axis=1)
+        if len(sources) > 1:
+            ens, wtd, inn = (jnp.concatenate(p, axis=1) for p in (ens, wtd, inn))
+        else:
+            ens, wtd, inn = ens[0], wtd[0], inn[0]
         grams.append(0.5 * (dot(wtd, ens, NT) + dot(ens, wtd, NT)))
         forces.append(dot(inn, wtd, NT)[0:1])
+    grams = [grams[c] + 0.5 * grams[1 - c] for c in range(2)]
+    forces = [forces[c] + 0.5 * forces[1 - c] for c in range(2)]
+    return grams, forces
+
+
+def gram_kernel(own_ref, mate_ref, system_ref, force_ref):
+    members = system_ref.shape[1]
+    grams, forces = tapered([(own_ref, 1.0), (mate_ref, 0.5)], members)
     spread = (members - 1) * eye(members, members)
-    systems = [spread + (grams[c] + 0.5 * grams[1 - c]) for c in range(2)]
-    forces = [forces[c] + 0.5 * forces[1 - c] for c in range(2)]
+    for c in range(2):
+        system_ref[c] = spread + grams[c]
+        force_ref[c] = forces[c]
+
+
+def update_kernel(system_ref, force_ref, far_ref, anom_ref, avg_ref, out_ref):
+    members = anom_ref.shape[1]
+    groups = members // 32
+    grams, forces = tapered([(far_ref, 0.5)], members)
+    systems = [system_ref[c] + grams[c] for c in range(2)]
+    forces = [force_ref[c] + forces[c] for c in range(2)]
     tops = invert128([s[:128, :128] for s in systems])
     across = [dot_full(t, s[:128, 128:]) for t, s in zip(tops, systems)]
     down = [dot_full(s[128:, :128], t, NT) for t, s in zip(tops, systems)]
@@ -239,14 +305,35 @@
     cells = level_count * TILE_WIDTH
     slots = measured_position.shape[2]
     chunk = (line_total, 16, 128)
-    wide = [pltpu.VMEM((line_total * 16, 128), F32)]
-
-    parted = call(split_kernel, jax.ShapeDtypeStruct(chunk, BF16), scratch=wide)(
-        prior_sample.reshape(part * level_count * width, line_total)
-    )
+    half = part * level_count * width // 2
+    scratch = [
+        pltpu.VMEM((PIECES, 2, half // PIECES, line_total), BF16),
+        pltpu.VMEM((line_total * 16, 128), F32),
+        pltpu.SemaphoreType.DMA((PIECES,)),
+    ]
+    rows = [int(r) for r in row_of(np.arange(line_total))]
+    device = {r: d for d, r in enumerate(rows)}
+    to_owner = [(r, device[r]) for r in range(line_total)]
+    to_mate = [(device[r], device[r ^ 1]) for r in range(line_total)]
+    to_far = [(device[r], device[r + 1]) for r in range(1, line_total - 1, 2)]
+    to_far = to_far + [(b, a) for a, b in to_far]
+
+    vmem = pl.BlockSpec(memory_space=pltpu.VMEM)
+    anywhere = pl.BlockSpec(memory_space=pl.ANY)
+    parted, observed = call(
+        split_kernel,
+        (jax.ShapeDtypeStruct(chunk, BF16), jax.ShapeDtypeStruct((8, slots), F32)),
+        in_specs=[anywhere, vmem, vmem, vmem, pl.BlockSpec(memory_space=pltpu.SMEM)],
+        scratch=scratch,
+    )(
+        prior_sample.reshape(2, half, line_total),
+        measured_position[0],
+        measured_datum[0],
+        measured_noise_spread[0],
+        measured_tally,
+    )
+    observed = lax.ppermute(observed, MEM, to_owner)
     relaid = lax.all_to_all(parted, MEM, split_axis=0, concat_axis=0, tiled=True)
-
-    vmem = pl.BlockSpec(memory_space=pltpu.VMEM)
     anomaly, average, packed = call(
         observe_kernel,
         (
@@ -254,28 +341,31 @@
             jax.ShapeDtypeStruct((2, 1, cells), F32),
             jax.ShapeDtypeStruct((2, members + 16, slots), BF16),
         ),
-        in_specs=[vmem, vmem, vmem, vmem, pl.BlockSpec(memory_space=pltpu.SMEM)],
-    )(
-        relaid.reshape(groups, tiles // 2, 2, 16, 128),
-        measured_position[0],
-        measured_datum[0],
-        measured_noise_spread[0],
-        measured_tally,
-    )
-    ends = line_total - 1
-    above = lax.ppermute(packed, MEM, [(i, i + 1) for i in range(ends)])
-    below = lax.ppermute(packed, MEM, [(i + 1, i) for i in range(ends)])
+    )(relaid.reshape(groups, tiles // 2, 2, 16, 128), observed)
+    far = lax.ppermute(packed, MEM, to_far)
+    mate = lax.ppermute(packed, MEM, to_mate)
+    system, force = call(
+        gram_kernel,
+        (
+            jax.ShapeDtypeStruct((2, members, members), F32),
+            jax.ShapeDtypeStruct((2, 1, members), F32),
+        ),
+        cost=pl.CostEstimate(
+            flops=16 * members * members * slots, bytes_accessed=2**21, transcendentals=0
+        ),
+    )(packed, mate)
     analyzed = call(
         update_kernel,
         jax.ShapeDtypeStruct((groups, tiles // 2, 2, 16, 128), BF16),
-    )(packed, above, below, anomaly, average)
+    )(system, force, far, anomaly, average)
     returned = lax.all_to_all(
         analyzed.reshape(chunk), MEM, split_axis=0, concat_axis=0, tiled=True
     )
     merged = call(
         merge_kernel,
-        jax.ShapeDtypeStruct((part * level_count * width, line_total), BF16),
-        scratch=wide,
+        jax.ShapeDtypeStruct((2, half, line_total), BF16),
+        out_specs=anywhere,
+        scratch=scratch,
     )(returned)
     return merged.reshape(part, level_count, width, line_total)
 

time: 120 us -> 115 us (0.958)
  blocking collectives: 83 us -> 38.5 us
  starting transfers between devices: 5.85 us -> 24.1 us
  waiting for transfers between devices: 11.9 us -> 30.1 us
  Pallas kernels: 17.6 us -> 20 us
    all_to_all x1 -> x0, blocking collectives: 46.6 us -> none  [on_device(): lax.all_to_all(parted, MEM, split_axis=0, concat_axis=0, tiled=True)]
    all_to_all x0 -> x1, waiting for transfers between devices: none -> 25.2 us  [on_device(): lax.all_to_all(parted, MEM, split_axis=0, concat_axis=0, tiled=True)]
    all_to_all x0 -> x1, starting transfers between devices: none -> 15.7 us  [on_device(): lax.all_to_all(parted, MEM, split_axis=0, concat_axis=0, tiled=True)]
    ppermute x2 -> x3, waiting for transfers between devices: 11.9 us -> 4.9 us  [the longest x1 4.13 us: on_device(): far = lax.ppermute(packed, MEM, to_far)]
    pallas_call x2 -> x3, Pallas kernels: 2.99 us -> 6.31 us  [the longest x1 3.35 us: on_device(): call(split_kernel, (jax.ShapeDtypeStruct(chunk, BF16), jax.ShapeDtypeStru...]
    ppermute x2 -> x3, starting transfers between devices: 5.85 us -> 8.48 us  [the longest x1 5.05 us: on_device(): observed = lax.ppermute(observed, MEM, to_owner)]
    all_to_all x1, blocking collectives: 36.3 us -> 38.5 us  [on_device(): lax.all_to_all(analyzed.reshape(chunk), MEM, split_axis=0, concat_axis=0,...]
  transfers between devices with their start and end apart: 2 -> 4, of which waited for: 2 -> 3; matrix products, arithmetic and copies ran while one was open for 0% -> 0% of each run, Pallas kernels for 0% -> 1%
where the time goes in v1:
time: 115 us
  blocking collectives  38.5 us (33%)
  waiting for transfers between devices  30.1 us (26%)
  starting transfers between devices  24.1 us (21%)
  Pallas kernels  20 us (17%)
  local copies, waits for them, and re-layouts  1.92 us (2%)
    all_to_all x1, blocking collectives, on_device(): lax.all_to_all(analyzed.reshape(chunk), MEM, split_axis=0, concat_axis=0,...  38.5 us
    all_to_all x1, waiting for transfers between devices, on_device(): lax.all_to_all(parted, MEM, split_axis=0, concat_axis=0, tiled=True)  25.2 us
    all_to_all x1, starting transfers between devices, on_device(): lax.all_to_all(parted, MEM, split_axis=0, concat_axis=0, tiled=True)  15.7 us
    pallas_call x1, Pallas kernels, on_device(): call(update_kernel, jax.ShapeDtypeStruct((groups, tiles // 2, 2, 16, 128)...  12.3 us
    ppermute x1, starting transfers between devices, on_device(): observed = lax.ppermute(observed, MEM, to_owner)  5.05 us
    ppermute x1, waiting for transfers between devices, on_device(): far = lax.ppermute(packed, MEM, to_far)  4.13 us
    pallas_call x1, Pallas kernels, on_device(): call(split_kernel, (jax.ShapeDtypeStruct(chunk, BF16), jax.ShapeDtypeStru...  3.35 us
    ppermute x1, starting transfers between devices, on_device(): far = lax.ppermute(packed, MEM, to_far)  3.09 us
  transfers between devices with their start and end apart: 4, of which 3 were waited for; matrix products, arithmetic and copies ran while one was open for 0% of the time, Pallas kernels for 1%

profile of v1, /device:TPU:1, one launch (start us, length us, event | category | flops | bytes accessed | tf_op | source)
XLA Modules:
  0.0 114.9 jit_solution(13935621700780457456)
XLA Ops:
  0.0 0.0 copy-start.2
  0.0 0.0 copy-start.1
  0.0 0.0 copy-start.3
  0.0 0.0 copy-start.4
  0.0 0.7 copy-done.2
  0.7 0.0 copy-done.1
  0.7 0.0 copy-done.3
  0.7 0.0 copy-done.4
  0.7 0.0 copy-start
  0.7 1.2 %copy-done = bf16[32,8,8,256]{3,2,1,0:T(8,128)(2,1)S(1)} copy-done((bf16[32,8,8,256]{3,2,1,0:T(8,128)(2,1)S(1)}, bf16[32,8,8,256]{3,2,1,0:T(8,128)(2,1)}, u32[]{:S(2)}) %copy-start) | copy-done | bytes 1048600
  1.9 3.3 %shard_map.55 = (bf16[256,16,128]{2,1,0:T(8,128)(2,1)}, f32[8,256]{1,0:T(8,128)S(1)}) custom-call(bf16[2,1024,256]{2,1,0:T(8,128)(2,1)S(1)} %bitcast.9, s32[2,256]{1,0:T(2,128)S(1)} %bitcast.10, f32[2,256]{1,0:T(2,128)S(1)} %bitcast.11, bf16[2,256]{1,0:T(2,128)(2,1)S(1)} %bitcast.12, s32[1,2]{1,0:T(1,128)S(1)} %copy-done.4), custom_call_target="tpu_custom_call" | custom-call | tf_op jit(solution)/shard_map/pallas_call | solution.py:323
  5.3 15.7 %all-to-all-start = ((bf16[256,16,128]{2,1,0:T(8,128)(2,1)}), bf16[256,16,128]{2,1,0:T(8,128)(2,1)S(1)}, u32[]{:S(2)}, u32[]{:S(2)}) async-start(bf16[256,16,128]{2,1,0:T(8,128)(2,1)} %get-tuple-element.12), calls=%async_computation | async-start | bytes 2097152 | tf_op jit(solution)/shard_map/all_to_all | solution.py:336
  21.0 5.1 %collective-permute-start = (f32[8,256]{1,0:T(8,128)S(1)}, f32[8,256]{1,0:T(8,128)S(1)}, u32[]{:S(2)}, u32[]{:S(2)}) collective-permute-start(f32[8,256]{1,0:T(8,128)S(1)} %get-tuple-element.13), channel_id=1, source_target_pairs={{0,0},{1,32},{2,4},{3,36},{4,8},{5,40},{6,12},{7,44},{8,16},{9,48}... | collective-permute-start | bytes 24584 | tf_op jit(solution)/shard_map/ppermute | solution.py:335
  26.0 0.8 collective-permute-done.obs_ref
  26.8 25.2 %all-to-all-done = bf16[256,16,128]{2,1,0:T(8,128)(2,1)S(1)} async-done(((bf16[256,16,128]{2,1,0:T(8,128)(2,1)}), bf16[256,16,128]{2,1,0:T(8,128)(2,1)S(1)}, u32[]{:S(2)}, u32[]{:S(2)}) %all-to-all-start) | async-done | bytes 1048608 | tf_op jit(solution)/shard_map/all_to_all | solution.py:336
  52.0 1.3 %shard_map.56 = (bf16[2,256,1024]{2,1,0:T(8,128)(2,1)S(1)}, f32[2,1,1024]{2,1,0:T(1,128)S(1)}, bf16[2,272,256]{2,1,0:T(8,128)(2,1)S(1)}) custom-call(bf16[8,16,2,16,128]{4,3,2,1,0:T(8,128)(2,1)S(1)} %bitcast.7, f32[8,256]{1,0:T(8,128)S(1)} %collective-permute-done.obs_ref), custom_call_target="tpu_custom_call" | custom-call | tf_op jit(solution)/shard_map/pallas_call | solution.py:337
  53.4 0.3 collective-permute-start.1
  53.7 3.1 %collective-permute-start.2 = (bf16[2,272,256]{2,1,0:T(8,128)(2,1)S(1)}, bf16[2,272,256]{2,1,0:T(8,128)(2,1)S(1)}, u32[]{:S(2)}, u32[]{:S(2)}) collective-permute-start(bf16[2,272,256]{2,1,0:T(8,128)(2,1)S(1)} %get-tuple-element.14.own_ref), channel_id=1, source_target_pairs={{32,4},{36,8},{40,12},{44,16},{48,20},{52,24},{56,28},{60,29},{61,... | collective-permute-start | bytes 835592 | tf_op jit(solution)/shard_map/ppermute | solution.py:345
  56.8 0.0 collective-permute-done.1.mate_ref
  56.8 0.6 shard_map.57
  57.4 4.1 %collective-permute-done.2.far_ref = bf16[2,272,256]{2,1,0:T(8,128)(2,1)S(1)} collective-permute-done((bf16[2,272,256]{2,1,0:T(8,128)(2,1)S(1)}, bf16[2,272,256]{2,1,0:T(8,128)(2,1)S(1)}, u32[]{:S(2)}, u32[]{:S(2)}) %collective-permute-start.2) | collective-permute-done | bytes 278560 | tf_op jit(solution)/shard_map/ppermute | solution.py:345
  61.6 12.3 %shard_map.58 = bf16[8,16,2,16,128]{4,3,2,1,0:T(8,128)(2,1)S(1)} custom-call(f32[2,256,256]{2,1,0:T(8,128)S(1)} %get-tuple-element.15.system_ref, f32[2,1,256]{2,1,0:T(1,128)S(1)} %get-tuple-element.16.force_ref, bf16[2,272,256]{2,1,0:T(8,128)(2,1)S(1)} %collective-permute-done.2.far_ref, bf16[2,256,1024]{2,1,0:T(8,128)(2,1)S(1)} %get-tuple-element.17.anom_ref, ...), custom_call_target="tpu_custom_call" | custom-call | tf_op jit(solution)/shard_map/pallas_call | solution.py:357
  73.9 38.5 %all_to_all.10.x_ref = bf16[256,16,128]{2,1,0:T(8,128)(2,1)S(1)} all-to-all(bf16[256,16,128]{2,1,0:T(8,128)(2,1)S(1)} %bitcast.8), channel_id=1, replica_groups=mesh['mem'=8,'tile'=32] {'mem','tile'}, dimensions={0} | all-to-all | bytes 2097152 | tf_op jit(solution)/shard_map/all_to_all | solution.py:361
  112.4 2.3 %shard_map.59 = bf16[2,1024,256]{2,1,0:T(8,128)(2,1)} custom-call(bf16[256,16,128]{2,1,0:T(8,128)(2,1)S(1)} %all_to_all.10.x_ref), custom_call_target="tpu_custom_call" | custom-call | tf_op jit(solution)/shard_map/pallas_call | solution.py:364
Async XLA Ops:
  0.0 0.7 copy-start.2
  0.0 0.7 copy-start.1
  0.0 0.7 copy-start.3
  0.0 0.7 copy-start.4
  0.7 1.2 %copy-start = (bf16[32,8,8,256]{3,2,1,0:T(8,128)(2,1)S(1)}, bf16[32,8,8,256]{3,2,1,0:T(8,128)(2,1)}, u32[]{:S(2)}) copy-start(bf16[32,8,8,256]{3,2,1,0:T(8,128)(2,1)} %param.5) | copy-start | bytes 3145732
  5.3 46.7 %all-to-all-start = ((bf16[256,16,128]{2,1,0:T(8,128)(2,1)}), bf16[256,16,128]{2,1,0:T(8,128)(2,1)S(1)}, u32[]{:S(2)}, u32[]{:S(2)}) async-start(bf16[256,16,128]{2,1,0:T(8,128)(2,1)} %get-tuple-element.12), calls=%async_computation | async-start | bytes 2097152 | tf_op jit(solution)/shard_map/all_to_all | solution.py:336
  21.0 5.8 %collective-permute-start = (f32[8,256]{1,0:T(8,128)S(1)}, f32[8,256]{1,0:T(8,128)S(1)}, u32[]{:S(2)}, u32[]{:S(2)}) collective-permute-start(f32[8,256]{1,0:T(8,128)S(1)} %get-tuple-element.13), channel_id=1, source_target_pairs={{0,0},{1,32},{2,4},{3,36},{4,8},{5,40},{6,12},{7,44},{8,16},{9,48}... | collective-permute-start | bytes 24584 | tf_op jit(solution)/shard_map/ppermute | solution.py:335
  53.4 3.4 %collective-permute-start.1 = (bf16[2,272,256]{2,1,0:T(8,128)(2,1)S(1)}, bf16[2,272,256]{2,1,0:T(8,128)(2,1)S(1)}, u32[]{:S(2)}, u32[]{:S(2)}) collective-permute-start(bf16[2,272,256]{2,1,0:T(8,128)(2,1)S(1)} %get-tuple-element.14.own_ref), channel_id=1, source_target_pairs={{0,32},{32,0},{4,36},{36,4},{8,40},{40,8},{12,44},{44,12},{16,48},... | collective-permute-start | bytes 835592 | tf_op jit(solution)/shard_map/ppermute | solution.py:346
  53.7 7.9 %collective-permute-start.2 = (bf16[2,272,256]{2,1,0:T(8,128)(2,1)S(1)}, bf16[2,272,256]{2,1,0:T(8,128)(2,1)S(1)}, u32[]{:S(2)}, u32[]{:S(2)}) collective-permute-start(bf16[2,272,256]{2,1,0:T(8,128)(2,1)S(1)} %get-tuple-element.14.own_ref), channel_id=1, source_target_pairs={{32,4},{36,8},{40,12},{44,16},{48,20},{52,24},{56,28},{60,29},{61,... | collective-permute-start | bytes 835592 | tf_op jit(solution)/shard_map/ppermute | solution.py:345

commit v2 on v1

--- a/solution.py
+++ b/solution.py
@@ -27,7 +27,7 @@
     )
 
 
-def call(body, out_shape, in_specs=None, out_specs=None, scratch=(), cost=None):
+def call(body, out_shape, in_specs=None, out_specs=None, scratch=(), cost=None, limit=VMEM_LIMIT):
     extra = {} if in_specs is None else {"in_specs": in_specs}
     if out_specs is not None:
         extra["out_specs"] = out_specs
@@ -36,7 +36,7 @@
         out_shape=out_shape,
         scratch_shapes=scratch,
         cost_estimate=cost,
-        compiler_params=pltpu.CompilerParams(vmem_limit_bytes=VMEM_LIMIT),
+        compiler_params=pltpu.CompilerParams(vmem_limit_bytes=limit),
         **extra,
     )
 
@@ -48,70 +48,57 @@
 
 
 def row_of(device):
-    x, core, z, y = device // 64, device // 32 % 2, device // 4 % 8, device % 4
-    along_y = y + (x % 2) * (3 - 2 * y)
-    along_z = z + (along_y % 2) * (7 - 2 * z)
+    x, core, z, y = device >> 6, (device >> 5) & 1, (device >> 2) & 7, device & 3
+    along_y = y + (x & 1) * (3 - 2 * y)
+    along_z = z + (along_y & 1) * (7 - 2 * z)
     return 2 * (x * 32 + along_y * 8 + along_z) + core
 
 
-def row_choice(total):
-    device = lax.broadcasted_iota(jnp.int32, (total, total), 0)
-    row = lax.broadcasted_iota(jnp.int32, (total, total), 1)
-    return jnp.where(row == row_of(device), 1.0, 0.0).astype(BF16)
-
-
-PIECES = 4
-
-
-def split_kernel(
-    x_ref, pos_ref, datum_ref, noise_ref, tally_ref, out_ref, obs_ref, held_ref, wide_ref, sems
-):
+PIECES = 8
+
+
+def split_kernel(x_ref, out_ref, wide_ref):
     rows = x_ref.shape[2]
-    span = x_ref.shape[1] // PIECES
-    copies = [
-        pltpu.make_async_copy(
-            x_ref.at[:, pl.ds(i * span, span), :], held_ref.at[i], sems.at[i]
+    owned = row_of(lax.broadcasted_iota(jnp.int32, (rows, 128), 0))
+    along = lax.broadcasted_iota(jnp.int32, (rows, 128), 1)
+    choice = jnp.concatenate(
+        [jnp.where(owned == along + r, 1.0, 0.0) for r in range(0, rows, 128)], axis=1
+    ).astype(BF16)
+    for g in range(16):
+        both = x_ref[:, g * 64 : (g + 1) * 64, :].reshape(128, rows)
+        wide_ref[pl.ds(g, rows, stride=16), :] = dot(choice, both, NT)
+    for d in range(0, rows, 32):
+        out_ref[d : d + 32] = (
+            wide_ref[d * 16 : (d + 32) * 16, :].astype(BF16).reshape(32, 16, 128)
         )
-        for i in range(PIECES)
-    ]
-    for copy in copies:
-        copy.start()
-    choice = row_choice(rows)
+
+
+def pack_kernel(pos_ref, datum_ref, noise_ref, tally_ref, obs_ref):
     slots = pos_ref.shape[1]
     pos = pos_ref[...]
-    level, col = pos // 128, pos % 128
-    obs_ref[0:2, :] = ((col // 8) * 64 + level * 8 + col % 8).astype(F32)
+    level, col = pos >> 7, pos & 127
+    obs_ref[0:2, :] = (((col >> 3) << 6) + (level << 3) + (col & 7)).astype(F32)
     obs_ref[2:4, :] = datum_ref[...]
     slot = lax.broadcasted_iota(jnp.int32, (1, slots), 1)
     for c in range(2):
         weights = 1.0 / noise_ref[c : c + 1, :].astype(F32)
         obs_ref[4 + c : 5 + c, :] = jnp.where(slot < tally_ref[0, c], weights, 0.0)
     obs_ref[6:8, :] = jnp.zeros((2, slots), F32)
-    for i in range(PIECES):
-        copies[i].wait()
-        for h in range(span // 64):
-            both = held_ref[i, :, h * 64 : (h + 1) * 64, :].reshape(128, rows)
-            g = i * (span // 64) + h
-            wide_ref[pl.ds(g, rows, stride=16), :] = dot(choice, both, NT)
-    for r in range(0, rows, 32):
-        out_ref[r : r + 32] = (
-            wide_ref[r * 16 : (r + 32) * 16, :].astype(BF16).reshape(32, 16, 128)
-        )
 
 
 def merge_kernel(x_ref, out_ref, held_ref, wide_ref, sems):
     rows = x_ref.shape[0]
     span = out_ref.shape[1] // PIECES
-    for r in range(0, rows, 32):
-        wide_ref[r * 16 : (r + 32) * 16, :] = x_ref[r : r + 32].reshape(32 * 16, 128).astype(F32)
-    choice = row_choice(rows)
+    for device in range(rows):
+        r = row_of(device)
+        wide_ref[r * 16 : (r + 1) * 16, :] = x_ref[device].astype(F32)
     unit = eye(128, 128).astype(BF16)
     copies = []
     for i in range(PIECES):
         for h in range(span // 64):
             g = i * (span // 64) + h
             part = wide_ref[pl.ds(g, rows, stride=16), :].astype(BF16)
-            turned = dot(dot(unit, part, NT).astype(BF16), choice).astype(BF16)
+            turned = dot(unit, part, NT).astype(BF16)
             held_ref[i, :, h * 64 : (h + 1) * 64, :] = turned.reshape(2, 64, rows)
         copy = pltpu.make_async_copy(
             held_ref.at[i], out_ref.at[:, pl.ds(i * span, span), :], sems.at[i]
@@ -168,71 +155,111 @@
 
 
 def invert64(rows):
-    n = rows[0].shape[0]
-    shape = (n, 8, 128)
-    sub = lax.broadcasted_iota(jnp.int32, shape, 1)
-
-    def lane(x, j):
-        return jnp.broadcast_to(x[:, :, j : j + 1], shape)
+    shape = rows[0].shape
+    sub = lax.broadcasted_iota(jnp.int32, shape, 0)
+    lane = lax.broadcasted_iota(jnp.int32, shape, 1)
+    half, own = lane & 64, lane & 63
+    unit = jnp.where((lane & 7) == sub, 1.0, 0.0)
+
+    def spread(x, col):
+        return jnp.take_along_axis(x, half + col, axis=1)
 
     def sublane(x, i):
-        return jnp.broadcast_to(x[:, i : i + 1, :], shape)
+        return jnp.broadcast_to(x[i : i + 1, :], shape)
 
     rows = list(rows)
+    following = [spread(rows[0], j) for j in range(8)]
     for b in range(8):
-        cols = {
-            (i, j): lane(rows[i], 64 + 8 * b + j) for i in range(b, 8) for j in range(8)
-        }
+        cols = {(b, j): following[j] for j in range(8)}
+        following = []
+        for i in range(b + 1, 8):
+            for j in range(8):
+                cols[i, j] = spread(rows[i], 8 * b + j)
+            if i == b + 1:
+                following = [spread(rows[i], 8 * i + j) for j in range(8)]
+        here = (own >> 3) == b
+        for i in range(b, 8):
+            rows[i] = jnp.where(here, unit if i == b else 0.0, rows[i])
         pivots = None
         for r in range(8):
             pivot = sublane(cols[b, r], r)
             pivots = pivot if r == 0 else jnp.where(sub == r, pivot, pivots)
             inverse = 1.0 / pivot
-            heads = {j: sublane(cols[b, j], r) for j in range(r + 1, 8)}
             factors = {}
             for i in range(b, 8):
                 factor = cols[i, r] * inverse
-                if i == b:
-                    factor = jnp.where(sub > r, factor, 0.0)
-                factors[i] = factor
-            for i in range(b, 8):
-                for j in range(r + 1, 8):
-                    cols[i, j] = cols[i, j] - factors[i] * heads[j]
+                factors[i] = jnp.where(sub > r, factor, 0.0) if i == b else factor
+            following = [
+                f - factors[b + 1] * sublane(cols[b + 1, r], j) for j, f in enumerate(following)
+            ]
+            for j in range(r + 1, 8):
+                head = sublane(cols[b, j], r)
+                for i in range(b, 8):
+                    cols[i, j] = cols[i, j] - factors[i] * head
             row = sublane(rows[b], r)
             for i in range(b, 8):
-                if i == b and r == 7:
-                    continue
-                rows[i] = rows[i] - factors[i] * row
-        rows[b] = rows[b] * lax.rsqrt(pivots)
+                if i > b or r < 7:
+                    rows[i] = rows[i] - factors[i] * row
+        rows[b] = jnp.where(own <= sub + 8 * b, rows[b] * lax.rsqrt(pivots), 0.0)
     return rows
 
 
-def invert128(systems):
-    n = len(systems)
+def invert256(systems):
     left = lax.broadcasted_iota(jnp.int32, (64, 128), 1) < 64
-    unit_left = eye(64, 128)
     unit_right = eye(64, 128, 64)
 
-    def run(blocks):
-        stack = [
-            jnp.stack([blk[8 * i : 8 * i + 8] for blk in blocks]) for i in range(8)
-        ]
-        done = invert64(stack)
-        return [jnp.concatenate([done[i][m] for i in range(8)], axis=0) for m in range(n)]
-
-    upper = [s[:64] for s in systems]
-    first = run([jnp.where(left, unit_left, pltpu.roll(u, 64, 1)) for u in upper])
-    tops = [jnp.where(left, f, 0.0) for f in first]
-    firsts = [f[:, :64] for f in first]
-    across = [dot_full(f, u) for f, u in zip(firsts, upper)]
-    down = [dot_full(s[64:, :64], f, NT) for s, f in zip(systems, firsts)]
-    lower = [s[64:] - dot_full(d, a) for s, d, a in zip(systems, down, across)]
-    second = run([jnp.where(left, unit_left, low) for low in lower])
-    joined = [
-        jnp.where(left, -dot_full(d, t), unit_right) for d, t in zip(down, tops)
+    def turn(x):
+        return pltpu.roll(x, 64, 1)
+
+    def run(pair, right):
+        low, high = pair
+        both = jnp.where(left, turn(low) if right else low, high if right else turn(high))
+        done = jnp.concatenate(invert64([both[8 * i : 8 * i + 8] for i in range(8)]), axis=0)
+        return [jnp.where(left, done, 0.0), jnp.where(left, turn(done), 0.0)]
+
+    first = run([s[:64, :128] for s in systems], False)
+    t0 = [t[:, :64] for t in first]
+    u0 = [dot_full(t, s[:64]) for t, s in zip(t0, systems)]
+    m0 = [dot_full(s[64:, :64], t, NT) for t, s in zip(t0, systems)]
+    s1 = [s[64:] - dot_full(m, u) for s, m, u in zip(systems, m0, u0)]
+
+    second = run([s[:64, :128] for s in s1], True)
+    t1 = [t[:, :64] for t in second]
+    u1 = [dot_full(t, s[:64, 128:]) for t, s in zip(t1, s1)]
+    m1 = [dot_full(s[64:, :128], turn(t), NT) for t, s in zip(second, s1)]
+    s2 = [s[64:, 128:] - dot_full(m, u) for s, m, u in zip(s1, m1, u1)]
+    l0 = first
+    l1 = [
+        dot_full(t, jnp.where(left, -dot_full(m[:64], p), unit_right))
+        for t, m, p in zip(t1, m0, l0)
     ]
-    bottoms = [dot_full(s[:, :64], j) for s, j in zip(second, joined)]
-    return [jnp.concatenate([t, b], axis=0) for t, b in zip(tops, bottoms)]
+
+    third = run([s[:64] for s in s2], False)
+    t2 = [t[:, :64] for t in third]
+    u2 = [dot_full(t, s[:64]) for t, s in zip(t2, s2)]
+    m2 = [dot_full(s[64:, :64], t, NT) for t, s in zip(t2, s2)]
+    s3 = [s[64:] - dot_full(m, u) for s, m, u in zip(s2, m2, u2)]
+    l2 = [
+        -dot_full(t, dot_full(m[64:128], p) + dot_full(n[:64], q))
+        for t, m, p, n, q in zip(t2, m0, l0, m1, l1)
+    ]
+    r3 = [
+        dot_full(m[128:], p) + dot_full(n[64:], q) + dot_full(o, z)
+        for m, p, n, q, o, z in zip(m0, l0, m1, l1, m2, l2)
+    ]
+    r3_right = [
+        jnp.where(left, -dot_full(o, z), unit_right) for o, z in zip(m2, third)
+    ]
+
+    fourth = run(s3, True)
+    t3 = [t[:, :64] for t in fourth]
+    rows = []
+    for c in range(2):
+        last = jnp.concatenate(
+            [-dot_full(t3[c], r3[c]), dot_full(t3[c], r3_right[c])], axis=1
+        )
+        rows.append([l0[c], l1[c], jnp.concatenate([l2[c], third[c]], axis=1), last])
+    return rows
 
 
 def tapered(sources, members):
@@ -273,20 +300,26 @@
     grams, forces = tapered([(far_ref, 0.5)], members)
     systems = [system_ref[c] + grams[c] for c in range(2)]
     forces = [force_ref[c] + forces[c] for c in range(2)]
-    tops = invert128([s[:128, :128] for s in systems])
-    across = [dot_full(t, s[:128, 128:]) for t, s in zip(tops, systems)]
-    down = [dot_full(s[128:, :128], t, NT) for t, s in zip(tops, systems)]
-    lower = [s[128:, 128:] - dot_full(d, a) for s, d, a in zip(systems, down, across)]
-    lows = invert128(lower)
-    mixed = [dot_full(d, t) for d, t in zip(down, tops)]
-    corners = [-dot_full(low, m) for low, m in zip(lows, mixed)]
-    for c in range(2):
-        top = jnp.concatenate([tops[c], jnp.zeros((128, 128), F32)], axis=1)
-        bottom = jnp.concatenate([corners[c], lows[c]], axis=1)
-        inverse = jnp.concatenate([top, bottom], axis=0)
-        halfway = jnp.sum(inverse * forces[c], axis=1, keepdims=True)
-        mean_weight = jnp.sum(inverse * halfway, axis=0, keepdims=True)
-        mixing = (math.sqrt(members - 1) * inverse + mean_weight).astype(BF16)
+    inverses = invert256(systems)
+    for c in range(2):
+        force = forces[c]
+        mean_weight = jnp.zeros((1, members), F32)
+        for rows in inverses[c]:
+            if rows.shape[1] < members:
+                halfway = jnp.sum(rows * force[:, :128], axis=1, keepdims=True)
+                part = jnp.sum(rows * halfway, axis=0, keepdims=True)
+                part = jnp.concatenate([part, jnp.zeros((1, 128), F32)], axis=1)
+            else:
+                halfway = jnp.sum(rows * force, axis=1, keepdims=True)
+                part = jnp.sum(rows * halfway, axis=0, keepdims=True)
+            mean_weight = mean_weight + part
+        scale = math.sqrt(members - 1)
+        mixing = []
+        for rows in inverses[c]:
+            if rows.shape[1] < members:
+                rows = jnp.concatenate([rows, jnp.zeros((64, 128), F32)], axis=1)
+            mixing.append((scale * rows + mean_weight).astype(BF16))
+        mixing = jnp.concatenate(mixing, axis=0)
         for tp in range(8):
             span = slice(tp * 128, (tp + 1) * 128)
             made = dot(mixing, anom_ref[c, :, span]) + avg_ref[c, :, span]
@@ -319,19 +352,17 @@
     to_far = to_far + [(b, a) for a, b in to_far]
 
     vmem = pl.BlockSpec(memory_space=pltpu.VMEM)
-    anywhere = pl.BlockSpec(memory_space=pl.ANY)
-    parted, observed = call(
+    anywhere = pl.BlockSpec(memory_space=pltpu.HBM)
+    parted = call(
         split_kernel,
-        (jax.ShapeDtypeStruct(chunk, BF16), jax.ShapeDtypeStruct((8, slots), F32)),
-        in_specs=[anywhere, vmem, vmem, vmem, pl.BlockSpec(memory_space=pltpu.SMEM)],
-        scratch=scratch,
-    )(
-        prior_sample.reshape(2, half, line_total),
-        measured_position[0],
-        measured_datum[0],
-        measured_noise_spread[0],
-        measured_tally,
-    )
+        jax.ShapeDtypeStruct(chunk, BF16),
+        scratch=scratch[1:2],
+    )(prior_sample.reshape(2, half, line_total))
+    observed = call(
+        pack_kernel,
+        jax.ShapeDtypeStruct((8, slots), F32),
+        in_specs=[vmem, vmem, vmem, pl.BlockSpec(memory_space=pltpu.SMEM)],
+    )(measured_position[0], measured_datum[0], measured_noise_spread[0], measured_tally)
     observed = lax.ppermute(observed, MEM, to_owner)
     relaid = lax.all_to_all(parted, MEM, split_axis=0, concat_axis=0, tiled=True)
     anomaly, average, packed = call(

time: 115 us -> 109 us (0.948)
  Pallas kernels: 20 us -> 14.7 us
  waiting for transfers between devices: 30.1 us -> 28.9 us
    pallas_call x1, Pallas kernels: 12.3 us -> 8.36 us  [on_device(): call(update_kernel, jax.ShapeDtypeStruct((groups, tiles // 2, 2, 16, 128)...]
    all_to_all x1, waiting for transfers between devices: 25.2 us -> 23.9 us  [on_device(): lax.all_to_all(parted, MEM, split_axis=0, concat_axis=0, tiled=True)]
    pallas_call x1 -> x2, Pallas kernels: 3.35 us -> 2.64 us  [the longest x1 2.09 us: on_device(): call(split_kernel, jax.ShapeDtypeStruct(chunk, BF16), scratch=scratch[1:2])]
where the time goes in v2:
time: 109 us; the launch traced here: 108 us
  blocking collectives  38.5 us (35%)
  waiting for transfers between devices  28.9 us (27%)
  starting transfers between devices  24.1 us (22%)
  Pallas kernels  14.7 us (13%)
  local copies, waits for them, and re-layouts  1.91 us (2%)
    all_to_all x1, blocking collectives, on_device(): lax.all_to_all(analyzed.reshape(chunk), MEM, split_axis=0, concat_axis=0,...  38.5 us
    all_to_all x1, waiting for transfers between devices, on_device(): lax.all_to_all(parted, MEM, split_axis=0, concat_axis=0, tiled=True)  23.9 us
    all_to_all x1, starting transfers between devices, on_device(): lax.all_to_all(parted, MEM, split_axis=0, concat_axis=0, tiled=True)  15.7 us
    pallas_call x1, Pallas kernels, on_device(): call(update_kernel, jax.ShapeDtypeStruct((groups, tiles // 2, 2, 16, 128)...  8.36 us
    ppermute x1, starting transfers between devices, on_device(): observed = lax.ppermute(observed, MEM, to_owner)  5.05 us
    ppermute x1, waiting for transfers between devices, on_device(): far = lax.ppermute(packed, MEM, to_far)  4.13 us
    ppermute x1, starting transfers between devices, on_device(): far = lax.ppermute(packed, MEM, to_far)  3.09 us
  transfers between devices with their start and end apart: 4, of which 3 were waited for; matrix products, arithmetic and copies ran while one was open for 0% of the time, Pallas kernels for 1%

profile of v2, /device:TPU:1, one launch (start us, length us, event | category | flops | bytes accessed | tf_op | source)
XLA Modules:
  0.0 108.3 jit_solution(6709038782922752361)
XLA Ops:
  0.0 1.2 %copy-done = bf16[32,8,8,256]{3,2,1,0:T(8,128)(2,1)S(1)} copy-done((bf16[32,8,8,256]{3,2,1,0:T(8,128)(2,1)S(1)}, bf16[32,8,8,256]{3,2,1,0:T(8,128)(2,1)}, u32[]{:S(2)}) %copy-start) | copy-done | bytes 1048600
  1.2 2.1 %shard_map.55 = bf16[256,16,128]{2,1,0:T(8,128)(2,1)} custom-call(bf16[2,1024,256]{2,1,0:T(8,128)(2,1)S(1)} %bitcast.9), custom_call_target="tpu_custom_call" | custom-call | tf_op jit(solution)/shard_map/pallas_call | solution.py:356
  3.3 15.7 %all-to-all-start = ((bf16[256,16,128]{2,1,0:T(8,128)(2,1)}), bf16[256,16,128]{2,1,0:T(8,128)(2,1)S(1)}, u32[]{:S(2)}, u32[]{:S(2)}) async-start(bf16[256,16,128]{2,1,0:T(8,128)(2,1)} %shard_map.55), calls=%async_computation | async-start | bytes 2097152 | tf_op jit(solution)/shard_map/all_to_all | solution.py:367
  19.0 0.0 copy-start.2
  19.0 0.0 copy-start.1
  19.0 0.0 copy-start.3
  19.0 0.0 copy-start.4
  19.0 0.6 copy-done.2
  19.7 0.0 copy-done.1
  19.7 0.0 copy-done.3
  19.7 0.0 copy-done.4
  19.7 0.6 shard_map.56
  20.3 5.1 %collective-permute-start = (f32[8,256]{1,0:T(8,128)S(1)}, f32[8,256]{1,0:T(8,128)S(1)}, u32[]{:S(2)}, u32[]{:S(2)}) collective-permute-start(f32[8,256]{1,0:T(8,128)S(1)} %shard_map.56), channel_id=1, source_target_pairs={{0,0},{1,32},{2,4},{3,36},{4,8},{5,40},{6,12},{7,44},{8,16},{9,48}... | collective-permute-start | bytes 24584 | tf_op jit(solution)/shard_map/ppermute | solution.py:366
  25.3 0.8 collective-permute-done.obs_ref
  26.1 23.9 %all-to-all-done = bf16[256,16,128]{2,1,0:T(8,128)(2,1)S(1)} async-done(((bf16[256,16,128]{2,1,0:T(8,128)(2,1)}), bf16[256,16,128]{2,1,0:T(8,128)(2,1)S(1)}, u32[]{:S(2)}, u32[]{:S(2)}) %all-to-all-start) | async-done | bytes 1048608 | tf_op jit(solution)/shard_map/all_to_all | solution.py:367
  50.0 1.3 %shard_map.57 = (bf16[2,256,1024]{2,1,0:T(8,128)(2,1)S(1)}, f32[2,1,1024]{2,1,0:T(1,128)S(1)}, bf16[2,272,256]{2,1,0:T(8,128)(2,1)S(1)}) custom-call(bf16[8,16,2,16,128]{4,3,2,1,0:T(8,128)(2,1)S(1)} %bitcast.7, f32[8,256]{1,0:T(8,128)S(1)} %collective-permute-done.obs_ref), custom_call_target="tpu_custom_call" | custom-call | tf_op jit(solution)/shard_map/pallas_call | solution.py:368
  51.4 0.3 collective-permute-start.1
  51.7 3.1 %collective-permute-start.2 = (bf16[2,272,256]{2,1,0:T(8,128)(2,1)S(1)}, bf16[2,272,256]{2,1,0:T(8,128)(2,1)S(1)}, u32[]{:S(2)}, u32[]{:S(2)}) collective-permute-start(bf16[2,272,256]{2,1,0:T(8,128)(2,1)S(1)} %get-tuple-element.10.own_ref), channel_id=1, source_target_pairs={{32,4},{36,8},{40,12},{44,16},{48,20},{52,24},{56,28},{60,29},{61,... | collective-permute-start | bytes 835592 | tf_op jit(solution)/shard_map/ppermute | solution.py:376
  54.8 0.0 collective-permute-done.1.mate_ref
  54.8 0.6 shard_map.58
  55.4 4.1 %collective-permute-done.2.far_ref = bf16[2,272,256]{2,1,0:T(8,128)(2,1)S(1)} collective-permute-done((bf16[2,272,256]{2,1,0:T(8,128)(2,1)S(1)}, bf16[2,272,256]{2,1,0:T(8,128)(2,1)S(1)}, u32[]{:S(2)}, u32[]{:S(2)}) %collective-permute-start.2) | collective-permute-done | bytes 278560 | tf_op jit(solution)/shard_map/ppermute | solution.py:376
  59.6 8.4 %shard_map.59 = bf16[8,16,2,16,128]{4,3,2,1,0:T(8,128)(2,1)S(1)} custom-call(f32[2,256,256]{2,1,0:T(8,128)S(1)} %get-tuple-element.11.system_ref, f32[2,1,256]{2,1,0:T(1,128)S(1)} %get-tuple-element.12.force_ref, bf16[2,272,256]{2,1,0:T(8,128)(2,1)S(1)} %collective-permute-done.2.far_ref, bf16[2,256,1024]{2,1,0:T(8,128)(2,1)S(1)} %get-tuple-element.13.anom_ref, ...), custom_call_target="tpu_custom_call" | custom-call | tf_op jit(solution)/shard_map/pallas_call | solution.py:388
  67.9 38.5 %all_to_all.10.x_ref = bf16[256,16,128]{2,1,0:T(8,128)(2,1)S(1)} all-to-all(bf16[256,16,128]{2,1,0:T(8,128)(2,1)S(1)} %bitcast.8), channel_id=1, replica_groups=mesh['mem'=8,'tile'=32] {'mem','tile'}, dimensions={0} | all-to-all | bytes 2097152 | tf_op jit(solution)/shard_map/all_to_all | solution.py:392
  106.4 1.8 %shard_map.60 = bf16[2,1024,256]{2,1,0:T(8,128)(2,1)} custom-call(bf16[256,16,128]{2,1,0:T(8,128)(2,1)S(1)} %all_to_all.10.x_ref), custom_call_target="tpu_custom_call" | custom-call | tf_op jit(solution)/shard_map/pallas_call | solution.py:395
  (1 shorter events, 0.0 us)
Async XLA Ops:
  0.0 1.2 %copy-start = (bf16[32,8,8,256]{3,2,1,0:T(8,128)(2,1)S(1)}, bf16[32,8,8,256]{3,2,1,0:T(8,128)(2,1)}, u32[]{:S(2)}) copy-start(bf16[32,8,8,256]{3,2,1,0:T(8,128)(2,1)} %param.5) | copy-start | bytes 3145732
  3.3 46.7 %all-to-all-start = ((bf16[256,16,128]{2,1,0:T(8,128)(2,1)}), bf16[256,16,128]{2,1,0:T(8,128)(2,1)S(1)}, u32[]{:S(2)}, u32[]{:S(2)}) async-start(bf16[256,16,128]{2,1,0:T(8,128)(2,1)} %shard_map.55), calls=%async_computation | async-start | bytes 2097152 | tf_op jit(solution)/shard_map/all_to_all | solution.py:367
  19.0 0.7 copy-start.2
  19.0 0.7 copy-start.1
  19.0 0.7 copy-start.3
  19.0 0.7 copy-start.4
  20.3 5.8 %collective-permute-start = (f32[8,256]{1,0:T(8,128)S(1)}, f32[8,256]{1,0:T(8,128)S(1)}, u32[]{:S(2)}, u32[]{:S(2)}) collective-permute-start(f32[8,256]{1,0:T(8,128)S(1)} %shard_map.56), channel_id=1, source_target_pairs={{0,0},{1,32},{2,4},{3,36},{4,8},{5,40},{6,12},{7,44},{8,16},{9,48}... | collective-permute-start | bytes 24584 | tf_op jit(solution)/shard_map/ppermute | solution.py:366
  51.4 3.4 %collective-permute-start.1 = (bf16[2,272,256]{2,1,0:T(8,128)(2,1)S(1)}, bf16[2,272,256]{2,1,0:T(8,128)(2,1)S(1)}, u32[]{:S(2)}, u32[]{:S(2)}) collective-permute-start(bf16[2,272,256]{2,1,0:T(8,128)(2,1)S(1)} %get-tuple-element.10.own_ref), channel_id=1, source_target_pairs={{0,32},{32,0},{4,36},{36,4},{8,40},{40,8},{12,44},{44,12},{16,48},... | collective-permute-start | bytes 835592 | tf_op jit(solution)/shard_map/ppermute | solution.py:377
  51.7 7.9 %collective-permute-start.2 = (bf16[2,272,256]{2,1,0:T(8,128)(2,1)S(1)}, bf16[2,272,256]{2,1,0:T(8,128)(2,1)S(1)}, u32[]{:S(2)}, u32[]{:S(2)}) collective-permute-start(bf16[2,272,256]{2,1,0:T(8,128)(2,1)S(1)} %get-tuple-element.10.own_ref), channel_id=1, source_target_pairs={{32,4},{36,8},{40,12},{44,16},{48,20},{52,24},{56,28},{60,29},{61,... | collective-permute-start | bytes 835592 | tf_op jit(solution)/shard_map/ppermute | solution.py:376

commit v3 on v2

--- a/solution.py
+++ b/solution.py
@@ -10,6 +10,7 @@
 
 TILE_WIDTH = 128
 MEM = ("mem", "tile")
+TILE_FIRST = ("tile", "mem")
 VMEM_LIMIT = 48 * 1024 * 1024
 F32 = jnp.float32
 BF16 = jnp.bfloat16
@@ -47,30 +48,44 @@
     return jnp.where(along == down + shift, 1.0, 0.0).astype(F32)
 
 
-def row_of(device):
-    x, core, z, y = device >> 6, (device >> 5) & 1, (device >> 2) & 7, device & 3
+def row_of(tile, mem):
+    x, core, z, y = mem >> 1, mem & 1, tile >> 2, tile & 3
     along_y = y + (x & 1) * (3 - 2 * y)
     along_z = z + (along_y & 1) * (7 - 2 * z)
     return 2 * (x * 32 + along_y * 8 + along_z) + core
 
 
+def row_of_chunk(chunk):
+    return row_of(chunk >> 3, chunk & 7)
+
+
 PIECES = 8
 
 
-def split_kernel(x_ref, out_ref, wide_ref):
+def split_kernel(x_ref, out_ref, held_ref, wide_ref, sems):
     rows = x_ref.shape[2]
-    owned = row_of(lax.broadcasted_iota(jnp.int32, (rows, 128), 0))
+    span = rows // PIECES
+    owned = row_of_chunk(lax.broadcasted_iota(jnp.int32, (rows, 128), 0))
     along = lax.broadcasted_iota(jnp.int32, (rows, 128), 1)
     choice = jnp.concatenate(
         [jnp.where(owned == along + r, 1.0, 0.0) for r in range(0, rows, 128)], axis=1
     ).astype(BF16)
-    for g in range(16):
-        both = x_ref[:, g * 64 : (g + 1) * 64, :].reshape(128, rows)
-        wide_ref[pl.ds(g, rows, stride=16), :] = dot(choice, both, NT)
-    for d in range(0, rows, 32):
-        out_ref[d : d + 32] = (
-            wide_ref[d * 16 : (d + 32) * 16, :].astype(BF16).reshape(32, 16, 128)
-        )
+    for g in range(0, 16, 2):
+        both = [
+            x_ref[:, h * 64 : (h + 1) * 64, :].reshape(128, rows) for h in (g, g + 1)
+        ]
+        both = dot(choice, jnp.concatenate(both, axis=0), NT)
+        wide_ref[pl.ds(g, rows, stride=16), :] = both[:, :128]
+        wide_ref[pl.ds(g + 1, rows, stride=16), :] = both[:, 128:]
+    copies = []
+    for i in range(PIECES):
+        d = i * span
+        held_ref[i] = wide_ref[d * 16 : (d + span) * 16, :].astype(BF16).reshape(span, 16, 128)
+        copy = pltpu.make_async_copy(held_ref.at[i], out_ref.at[pl.ds(d, span)], sems.at[i])
+        copy.start()
+        copies.append(copy)
+    for copy in copies:
+        copy.wait()
 
 
 def pack_kernel(pos_ref, datum_ref, noise_ref, tally_ref, obs_ref):
@@ -89,9 +104,9 @@
 def merge_kernel(x_ref, out_ref, held_ref, wide_ref, sems):
     rows = x_ref.shape[0]
     span = out_ref.shape[1] // PIECES
-    for device in range(rows):
-        r = row_of(device)
-        wide_ref[r * 16 : (r + 1) * 16, :] = x_ref[device].astype(F32)
+    for chunk in range(rows):
+        r = row_of_chunk(chunk)
+        wide_ref[r * 16 : (r + 1) * 16, :] = x_ref[chunk].astype(F32)
     unit = eye(128, 128).astype(BF16)
     copies = []
     for i in range(PIECES):
@@ -112,20 +127,19 @@
 def swap_halves(low, high):
     left = lax.broadcasted_iota(jnp.int32, low.shape, low.ndim - 1) < 64
     axis = low.ndim - 1
-    first = jnp.where(left, low, pltpu.roll(high, 64, axis))
-    second = jnp.where(left, pltpu.roll(low, 64, axis), high)
-    return first, second
+    inner = pltpu.roll(jnp.where(left, high, low), 64, axis)
+    return jnp.where(left, low, inner), jnp.where(left, inner, high)
 
 
 def observe_kernel(x_ref, obs_ref, anom_ref, avg_ref, pack_ref):
     members = anom_ref.shape[1]
-    groups = x_ref.shape[0]
+    groups = x_ref.shape[2]
     cell_total = anom_ref.shape[2]
     slots = pack_ref.shape[2]
     for c in range(2):
         for tp in range(8):
-            low = x_ref[:, c * 8 + tp, 0].astype(F32)
-            high = x_ref[:, c * 8 + tp, 1].astype(F32)
+            low = x_ref[c * 8 + tp, 0].astype(F32)
+            high = x_ref[c * 8 + tp, 1].astype(F32)
             first, second = swap_halves(low, high)
             cells = jnp.concatenate([first, second], axis=1).reshape(groups * 32, 128)
             average = jnp.sum(cells, axis=0, keepdims=True) / members
@@ -219,39 +233,40 @@
 
     first = run([s[:64, :128] for s in systems], False)
     t0 = [t[:, :64] for t in first]
-    u0 = [dot_full(t, s[:64]) for t, s in zip(t0, systems)]
-    m0 = [dot_full(s[64:, :64], t, NT) for t, s in zip(t0, systems)]
-    s1 = [s[64:] - dot_full(m, u) for s, m, u in zip(systems, m0, u0)]
-
-    second = run([s[:64, :128] for s in s1], True)
+    u0 = [dot_full(t, s[:64, :128]) for t, s in zip(t0, systems)]
+    m0 = [dot_full(s[64:128, :64], t, NT) for t, s in zip(t0, systems)]
+    s1 = [s[64:128, :128] - dot_full(m, u) for s, m, u in zip(systems, m0, u0)]
+
+    second = run(s1, True)
+    v0 = [dot_full(t, s[:64, 128:]) for t, s in zip(t0, systems)]
+    n0 = [dot_full(s[128:, :64], t, NT) for t, s in zip(t0, systems)]
+    up1 = [s[64:128, 128:] - dot_full(m, v) for s, m, v in zip(systems, m0, v0)]
+    down1 = [s[128:, :128] - dot_full(n, u) for s, n, u in zip(systems, n0, u0)]
+    rest = [s[128:, 128:] - dot_full(n, v) for s, n, v in zip(systems, n0, v0)]
     t1 = [t[:, :64] for t in second]
-    u1 = [dot_full(t, s[:64, 128:]) for t, s in zip(t1, s1)]
-    m1 = [dot_full(s[64:, :128], turn(t), NT) for t, s in zip(second, s1)]
-    s2 = [s[64:, 128:] - dot_full(m, u) for s, m, u in zip(s1, m1, u1)]
+    u1 = [dot_full(t, u) for t, u in zip(t1, up1)]
+    m1 = [dot_full(d, turn(t), NT) for t, d in zip(second, down1)]
+    s2 = [s[:64] - dot_full(m[:64], u) for s, m, u in zip(rest, m1, u1)]
+
+    third = run(s2, False)
+    low2 = [s[64:] - dot_full(m[64:], u) for s, m, u in zip(rest, m1, u1)]
     l0 = first
     l1 = [
-        dot_full(t, jnp.where(left, -dot_full(m[:64], p), unit_right))
+        dot_full(t, jnp.where(left, -dot_full(m, p), unit_right))
         for t, m, p in zip(t1, m0, l0)
     ]
-
-    third = run([s[:64] for s in s2], False)
+    r2 = [
+        dot_full(n, p) + dot_full(m, q) for n, p, m, q in zip(n0, l0, m1, l1)
+    ]
     t2 = [t[:, :64] for t in third]
-    u2 = [dot_full(t, s[:64]) for t, s in zip(t2, s2)]
-    m2 = [dot_full(s[64:, :64], t, NT) for t, s in zip(t2, s2)]
-    s3 = [s[64:] - dot_full(m, u) for s, m, u in zip(s2, m2, u2)]
-    l2 = [
-        -dot_full(t, dot_full(m[64:128], p) + dot_full(n[:64], q))
-        for t, m, p, n, q in zip(t2, m0, l0, m1, l1)
-    ]
-    r3 = [
-        dot_full(m[128:], p) + dot_full(n[64:], q) + dot_full(o, z)
-        for m, p, n, q, o, z in zip(m0, l0, m1, l1, m2, l2)
-    ]
-    r3_right = [
-        jnp.where(left, -dot_full(o, z), unit_right) for o, z in zip(m2, third)
-    ]
+    u2 = [dot_full(t, s) for t, s in zip(t2, s2)]
+    m2 = [dot_full(s[:, :64], t, NT) for t, s in zip(t2, low2)]
+    s3 = [s - dot_full(m, u) for s, m, u in zip(low2, m2, u2)]
 
     fourth = run(s3, True)
+    l2 = [-dot_full(t, r[:64]) for t, r in zip(t2, r2)]
+    r3 = [r[64:] + dot_full(m, p) for r, m, p in zip(r2, m2, l2)]
+    r3_right = [jnp.where(left, -dot_full(m, p), unit_right) for m, p in zip(m2, third)]
     t3 = [t[:, :64] for t in fourth]
     rows = []
     for c in range(2):
@@ -262,42 +277,42 @@
     return rows
 
 
-def tapered(sources, members):
+def tapered(refs, falloff, members):
     grams, forces = [], []
     for c in range(2):
         ens, wtd, inn = [], [], []
-        for ref, falloff in sources:
+        for ref in refs:
             ensemble = ref[c, :members, :]
             tail = ref[c, members:, :]
             weights = tail[1:2, :].astype(F32)
-            weighted = (weights * ensemble.astype(F32)).astype(BF16)
             ens.append(ensemble)
-            wtd.append((weighted.astype(F32) * falloff).astype(BF16))
+            wtd.append((weights * ensemble.astype(F32)).astype(BF16))
             inn.append(tail)
-        if len(sources) > 1:
+        if len(refs) > 1:
             ens, wtd, inn = (jnp.concatenate(p, axis=1) for p in (ens, wtd, inn))
         else:
             ens, wtd, inn = ens[0], wtd[0], inn[0]
-        grams.append(0.5 * (dot(wtd, ens, NT) + dot(ens, wtd, NT)))
-        forces.append(dot(inn, wtd, NT)[0:1])
+        grams.append(0.5 * falloff * (dot(wtd, ens, NT) + dot(ens, wtd, NT)))
+        forces.append(falloff * dot(inn, wtd, NT)[0:1])
     grams = [grams[c] + 0.5 * grams[1 - c] for c in range(2)]
     forces = [forces[c] + 0.5 * forces[1 - c] for c in range(2)]
     return grams, forces
 
 
-def gram_kernel(own_ref, mate_ref, system_ref, force_ref):
+def gram_kernel(own_ref, system_ref, force_ref, hand_ref):
     members = system_ref.shape[1]
-    grams, forces = tapered([(own_ref, 1.0), (mate_ref, 0.5)], members)
+    hand_ref[...] = own_ref[...]
+    grams, forces = tapered([own_ref], 1.0, members)
     spread = (members - 1) * eye(members, members)
     for c in range(2):
         system_ref[c] = spread + grams[c]
         force_ref[c] = forces[c]
 
 
-def update_kernel(system_ref, force_ref, far_ref, anom_ref, avg_ref, out_ref):
+def update_kernel(system_ref, force_ref, mate_ref, far_ref, anom_ref, avg_ref, out_ref):
     members = anom_ref.shape[1]
     groups = members // 32
-    grams, forces = tapered([(far_ref, 0.5)], members)
+    grams, forces = tapered([mate_ref, far_ref], 0.5, members)
     systems = [system_ref[c] + grams[c] for c in range(2)]
     forces = [force_ref[c] + forces[c] for c in range(2)]
     inverses = invert256(systems)
@@ -320,13 +335,14 @@
                 rows = jnp.concatenate([rows, jnp.zeros((64, 128), F32)], axis=1)
             mixing.append((scale * rows + mean_weight).astype(BF16))
         mixing = jnp.concatenate(mixing, axis=0)
-        for tp in range(8):
-            span = slice(tp * 128, (tp + 1) * 128)
+        for tp in range(0, 8, 2):
+            span = slice(tp * 128, (tp + 2) * 128)
             made = dot(mixing, anom_ref[c, :, span]) + avg_ref[c, :, span]
-            made = made.reshape(groups, 32, 128)
-            low, high = swap_halves(made[:, :16], made[:, 16:])
-            out_ref[:, c * 8 + tp, 0] = low.astype(BF16)
-            out_ref[:, c * 8 + tp, 1] = high.astype(BF16)
+            for h in range(2):
+                part = made[:, h * 128 : (h + 1) * 128].reshape(groups, 32, 128)
+                low, high = swap_halves(part[:, :16], part[:, 16:])
+                out_ref[c * 8 + tp + h, 0] = low.astype(BF16)
+                out_ref[c * 8 + tp + h, 1] = high.astype(BF16)
 
 
 def on_device(
@@ -338,13 +354,15 @@
     cells = level_count * TILE_WIDTH
     slots = measured_position.shape[2]
     chunk = (line_total, 16, 128)
+    paired = (tiles // 2, 2, groups, 16, 128)
     half = part * level_count * width // 2
     scratch = [
         pltpu.VMEM((PIECES, 2, half // PIECES, line_total), BF16),
         pltpu.VMEM((line_total * 16, 128), F32),
         pltpu.SemaphoreType.DMA((PIECES,)),
     ]
-    rows = [int(r) for r in row_of(np.arange(line_total))]
+    places = np.arange(line_total)
+    rows = [int(r) for r in row_of(places % tiles, places // tiles)]
     device = {r: d for d, r in enumerate(rows)}
     to_owner = [(r, device[r]) for r in range(line_total)]
     to_mate = [(device[r], device[r ^ 1]) for r in range(line_total)]
@@ -356,7 +374,8 @@
     parted = call(
         split_kernel,
         jax.ShapeDtypeStruct(chunk, BF16),
-        scratch=scratch[1:2],
+        out_specs=anywhere,
+        scratch=[pltpu.VMEM((PIECES, line_total // PIECES, 16, 128), BF16)] + scratch[1:],
     )(prior_sample.reshape(2, half, line_total))
     observed = call(
         pack_kernel,
@@ -364,7 +383,7 @@
         in_specs=[vmem, vmem, vmem, pl.BlockSpec(memory_space=pltpu.SMEM)],
     )(measured_position[0], measured_datum[0], measured_noise_spread[0], measured_tally)
     observed = lax.ppermute(observed, MEM, to_owner)
-    relaid = lax.all_to_all(parted, MEM, split_axis=0, concat_axis=0, tiled=True)
+    relaid = lax.all_to_all(parted, TILE_FIRST, split_axis=0, concat_axis=0, tiled=True)
     anomaly, average, packed = call(
         observe_kernel,
         (
@@ -372,25 +391,23 @@
             jax.ShapeDtypeStruct((2, 1, cells), F32),
             jax.ShapeDtypeStruct((2, members + 16, slots), BF16),
         ),
-    )(relaid.reshape(groups, tiles // 2, 2, 16, 128), observed)
+    )(relaid.reshape(paired), observed)
     far = lax.ppermute(packed, MEM, to_far)
-    mate = lax.ppermute(packed, MEM, to_mate)
-    system, force = call(
+    system, force, hand = call(
         gram_kernel,
         (
             jax.ShapeDtypeStruct((2, members, members), F32),
             jax.ShapeDtypeStruct((2, 1, members), F32),
+            jax.ShapeDtypeStruct(packed.shape, BF16),
         ),
-        cost=pl.CostEstimate(
-            flops=16 * members * members * slots, bytes_accessed=2**21, transcendentals=0
-        ),
-    )(packed, mate)
+    )(packed)
+    mate = lax.ppermute(hand, MEM, to_mate)
     analyzed = call(
         update_kernel,
-        jax.ShapeDtypeStruct((groups, tiles // 2, 2, 16, 128), BF16),
-    )(system, force, far, anomaly, average)
+        jax.ShapeDtypeStruct(paired, BF16),
+    )(system, force, mate, far, anomaly, average)
     returned = lax.all_to_all(
-        analyzed.reshape(chunk), MEM, split_axis=0, concat_axis=0, tiled=True
+        analyzed.reshape(chunk), TILE_FIRST, split_axis=0, concat_axis=0, tiled=True
     )
     merged = call(
         merge_kernel,

time: 109 us -> 106 us (0.972)
  waiting for transfers between devices: 28.9 us -> 27.8 us
    ppermute x1, starting transfers between devices: 3.09 us -> 4.32 us  [on_device(): far = lax.ppermute(packed, MEM, to_far)]
where the time goes in v3:
time: 106 us
  blocking collectives  37.5 us (35%)
  waiting for transfers between devices  27.8 us (26%)
  starting transfers between devices  25.1 us (24%)
  Pallas kernels  13.8 us (13%)
  local copies, waits for them, and re-layouts  1.91 us (2%)
    all_to_all x1, blocking collectives, on_device(): lax.all_to_all(analyzed.reshape(chunk), TILE_FIRST, split_axis=0, concat_...  37.5 us
    all_to_all x1, waiting for transfers between devices, on_device(): lax.all_to_all(parted, TILE_FIRST, split_axis=0, concat_axis=0, tiled=True)  23.3 us
    all_to_all x1, starting transfers between devices, on_device(): lax.all_to_all(parted, TILE_FIRST, split_axis=0, concat_axis=0, tiled=True)  15.7 us
    pallas_call x1, Pallas kernels, on_device(): call(update_kernel, jax.ShapeDtypeStruct(paired, BF16))  8.01 us
    ppermute x1, starting transfers between devices, on_device(): observed = lax.ppermute(observed, MEM, to_owner)  5.05 us
    ppermute x1, starting transfers between devices, on_device(): far = lax.ppermute(packed, MEM, to_far)  4.32 us
    ppermute x1, waiting for transfers between devices, on_device(): far = lax.ppermute(packed, MEM, to_far)  3.69 us
  transfers between devices with their start and end apart: 4, of which 3 were waited for; matrix products, arithmetic and copies ran while one was open for 0% of the time, Pallas kernels for 1%

profile of v3, /device:TPU:1, one launch (start us, length us, event | category | flops | bytes accessed | tf_op | source)
XLA Modules:
  0.0 106.2 jit_solution(9386733816661444472)
XLA Ops:
  0.0 1.2 %copy-done = bf16[32,8,8,256]{3,2,1,0:T(8,128)(2,1)S(1)} copy-done((bf16[32,8,8,256]{3,2,1,0:T(8,128)(2,1)S(1)}, bf16[32,8,8,256]{3,2,1,0:T(8,128)(2,1)}, u32[]{:S(2)}) %copy-start) | copy-done | bytes 1048600
  1.2 1.7 %shard_map.55 = bf16[256,16,128]{2,1,0:T(8,128)(2,1)} custom-call(bf16[2,1024,256]{2,1,0:T(8,128)(2,1)S(1)} %bitcast.9), custom_call_target="tpu_custom_call" | custom-call | tf_op jit(solution)/shard_map/pallas_call | solution.py:374
  3.0 15.7 %all-to-all-start = ((bf16[256,16,128]{2,1,0:T(8,128)(2,1)}), bf16[256,16,128]{2,1,0:T(8,128)(2,1)S(1)}, u32[]{:S(2)}, u32[]{:S(2)}) async-start(bf16[256,16,128]{2,1,0:T(8,128)(2,1)} %shard_map.55), calls=%async_computation | async-start | bytes 2097152 | tf_op jit(solution)/shard_map/all_to_all | solution.py:386
  18.7 0.0 copy-start.2
  18.7 0.0 copy-start.1
  18.7 0.0 copy-start.3
  18.7 0.0 copy-start.4
  18.7 0.6 copy-done.2
  19.3 0.0 copy-done.1
  19.4 0.0 copy-done.3
  19.4 0.0 copy-done.4
  19.4 0.6 shard_map.56
  19.9 5.1 %collective-permute-start = (f32[8,256]{1,0:T(8,128)S(1)}, f32[8,256]{1,0:T(8,128)S(1)}, u32[]{:S(2)}, u32[]{:S(2)}) collective-permute-start(f32[8,256]{1,0:T(8,128)S(1)} %shard_map.56), channel_id=1, source_target_pairs={{0,0},{1,32},{2,4},{3,36},{4,8},{5,40},{6,12},{7,44},{8,16},{9,48}... | collective-permute-start | bytes 24584 | tf_op jit(solution)/shard_map/ppermute | solution.py:385
  25.0 0.8 collective-permute-done.obs_ref
  25.8 23.3 %all-to-all-done = bf16[256,16,128]{2,1,0:T(8,128)(2,1)S(1)} async-done(((bf16[256,16,128]{2,1,0:T(8,128)(2,1)}), bf16[256,16,128]{2,1,0:T(8,128)(2,1)S(1)}, u32[]{:S(2)}, u32[]{:S(2)}) %all-to-all-start) | async-done | bytes 1048608 | tf_op jit(solution)/shard_map/all_to_all | solution.py:386
  49.1 1.3 %shard_map.57 = (bf16[2,256,1024]{2,1,0:T(8,128)(2,1)S(1)}, f32[2,1,1024]{2,1,0:T(1,128)S(1)}, bf16[2,272,256]{2,1,0:T(8,128)(2,1)S(1)}) custom-call(bf16[16,2,8,16,128]{4,3,2,1,0:T(8,128)(2,1)S(1)} %bitcast.7, f32[8,256]{1,0:T(8,128)S(1)} %collective-permute-done.obs_ref), custom_call_target="tpu_custom_call" | custom-call | tf_op jit(solution)/shard_map/pallas_call | solution.py:387
  50.4 4.3 %collective-permute-start.2 = (bf16[2,272,256]{2,1,0:T(8,128)(2,1)S(1)}, bf16[2,272,256]{2,1,0:T(8,128)(2,1)S(1)}, u32[]{:S(2)}, u32[]{:S(2)}) collective-permute-start(bf16[2,272,256]{2,1,0:T(8,128)(2,1)S(1)} %get-tuple-element.11.own_ref), channel_id=1, source_target_pairs={{32,4},{36,8},{40,12},{44,16},{48,20},{52,24},{56,28},{60,29},{61,... | collective-permute-start | bytes 835592 | tf_op jit(solution)/shard_map/ppermute | solution.py:395
  54.7 0.4 shard_map.58
  55.1 0.1 collective-permute-start.1
  55.2 3.7 %collective-permute-done.2.far_ref = bf16[2,272,256]{2,1,0:T(8,128)(2,1)S(1)} collective-permute-done((bf16[2,272,256]{2,1,0:T(8,128)(2,1)S(1)}, bf16[2,272,256]{2,1,0:T(8,128)(2,1)S(1)}, u32[]{:S(2)}, u32[]{:S(2)}) %collective-permute-start.2) | collective-permute-done | bytes 278560 | tf_op jit(solution)/shard_map/ppermute | solution.py:395
  58.9 0.0 collective-permute-done.1.mate_ref
  58.9 8.0 %shard_map.59 = bf16[16,2,8,16,128]{4,3,2,1,0:T(8,128)(2,1)S(1)} custom-call(f32[2,256,256]{2,1,0:T(8,128)S(1)} %get-tuple-element.12.system_ref, f32[2,1,256]{2,1,0:T(1,128)S(1)} %get-tuple-element.13.force_ref, bf16[2,272,256]{2,1,0:T(8,128)(2,1)S(1)} %collective-permute-done.1.mate_ref, bf16[2,272,256]{2,1,0:T(8,128)(2,1)S(1)} %collective-permute-done.2.far_ref, ...), custom_call_target="tpu_custom_call" | custom-call | tf_op jit(solution)/shard_map/pallas_call | solution.py:405
  67.0 37.5 %all_to_all.10.x_ref = bf16[256,16,128]{2,1,0:T(8,128)(2,1)S(1)} all-to-all(bf16[256,16,128]{2,1,0:T(8,128)(2,1)S(1)} %bitcast.8), channel_id=1, replica_groups=mesh['mem'=8,'tile'=32] {'tile','mem'}, dimensions={0} | all-to-all | bytes 2097152 | tf_op jit(solution)/shard_map/all_to_all | solution.py:409
  104.4 1.8 %shard_map.60 = bf16[2,1024,256]{2,1,0:T(8,128)(2,1)} custom-call(bf16[256,16,128]{2,1,0:T(8,128)(2,1)S(1)} %all_to_all.10.x_ref), custom_call_target="tpu_custom_call" | custom-call | tf_op jit(solution)/shard_map/pallas_call | solution.py:412
  (1 shorter events, 0.0 us)
Async XLA Ops:
  0.0 1.2 %copy-start = (bf16[32,8,8,256]{3,2,1,0:T(8,128)(2,1)S(1)}, bf16[32,8,8,256]{3,2,1,0:T(8,128)(2,1)}, u32[]{:S(2)}) copy-start(bf16[32,8,8,256]{3,2,1,0:T(8,128)(2,1)} %param.5) | copy-start | bytes 3145732
  3.0 46.1 %all-to-all-start = ((bf16[256,16,128]{2,1,0:T(8,128)(2,1)}), bf16[256,16,128]{2,1,0:T(8,128)(2,1)S(1)}, u32[]{:S(2)}, u32[]{:S(2)}) async-start(bf16[256,16,128]{2,1,0:T(8,128)(2,1)} %shard_map.55), calls=%async_computation | async-start | bytes 2097152 | tf_op jit(solution)/shard_map/all_to_all | solution.py:386
  18.7 0.7 copy-start.2
  18.7 0.7 copy-start.1
  18.7 0.7 copy-start.3
  18.7 0.7 copy-start.4
  19.9 5.8 %collective-permute-start = (f32[8,256]{1,0:T(8,128)S(1)}, f32[8,256]{1,0:T(8,128)S(1)}, u32[]{:S(2)}, u32[]{:S(2)}) collective-permute-start(f32[8,256]{1,0:T(8,128)S(1)} %shard_map.56), channel_id=1, source_target_pairs={{0,0},{1,32},{2,4},{3,36},{4,8},{5,40},{6,12},{7,44},{8,16},{9,48}... | collective-permute-start | bytes 24584 | tf_op jit(solution)/shard_map/ppermute | solution.py:385
  50.4 8.5 %collective-permute-start.2 = (bf16[2,272,256]{2,1,0:T(8,128)(2,1)S(1)}, bf16[2,272,256]{2,1,0:T(8,128)(2,1)S(1)}, u32[]{:S(2)}, u32[]{:S(2)}) collective-permute-start(bf16[2,272,256]{2,1,0:T(8,128)(2,1)S(1)} %get-tuple-element.11.own_ref), channel_id=1, source_target_pairs={{32,4},{36,8},{40,12},{44,16},{48,20},{52,24},{56,28},{60,29},{61,... | collective-permute-start | bytes 835592 | tf_op jit(solution)/shard_map/ppermute | solution.py:395
  55.1 3.8 %collective-permute-start.1 = (bf16[2,272,256]{2,1,0:T(8,128)(2,1)S(1)}, bf16[2,272,256]{2,1,0:T(8,128)(2,1)S(1)}, u32[]{:S(2)}, u32[]{:S(2)}) collective-permute-start(bf16[2,272,256]{2,1,0:T(8,128)(2,1)S(1)} %get-tuple-element.14), channel_id=1, source_target_pairs={{0,32},{32,0},{4,36},{36,4},{8,40},{40,8},{12,44},{44,12},{16,48},... | collective-permute-start | bytes 835592 | tf_op jit(solution)/shard_map/ppermute | solution.py:404

commit v4 on v3

--- a/solution.py
+++ b/solution.py
@@ -208,7 +208,8 @@
             ]
             for j in range(r + 1, 8):
                 head = sublane(cols[b, j], r)
-                for i in range(b, 8):
+                cols[b, j] = cols[b, j] - (cols[b, r] * head) * inverse
+                for i in range(b + 1, 8):
                     cols[i, j] = cols[i, j] - factors[i] * head
             row = sublane(rows[b], r)
             for i in range(b, 8):
@@ -218,91 +219,107 @@
     return rows
 
 
-def invert256(systems):
+def invert256(systems, low, high):
     left = lax.broadcasted_iota(jnp.int32, (64, 128), 1) < 64
     unit_right = eye(64, 128, 64)
 
     def turn(x):
         return pltpu.roll(x, 64, 1)
 
-    def run(pair, right):
-        low, high = pair
-        both = jnp.where(left, turn(low) if right else low, high if right else turn(high))
+    def run(low, high):
+        both = jnp.where(left, low, high)
         done = jnp.concatenate(invert64([both[8 * i : 8 * i + 8] for i in range(8)]), axis=0)
-        return [jnp.where(left, done, 0.0), jnp.where(left, turn(done), 0.0)]
-
-    first = run([s[:64, :128] for s in systems], False)
-    t0 = [t[:, :64] for t in first]
-    u0 = [dot_full(t, s[:64, :128]) for t, s in zip(t0, systems)]
-    m0 = [dot_full(s[64:128, :64], t, NT) for t, s in zip(t0, systems)]
-    s1 = [s[64:128, :128] - dot_full(m, u) for s, m, u in zip(systems, m0, u0)]
-
-    second = run(s1, True)
-    v0 = [dot_full(t, s[:64, 128:]) for t, s in zip(t0, systems)]
-    n0 = [dot_full(s[128:, :64], t, NT) for t, s in zip(t0, systems)]
-    up1 = [s[64:128, 128:] - dot_full(m, v) for s, m, v in zip(systems, m0, v0)]
-    down1 = [s[128:, :128] - dot_full(n, u) for s, n, u in zip(systems, n0, u0)]
-    rest = [s[128:, 128:] - dot_full(n, v) for s, n, v in zip(systems, n0, v0)]
-    t1 = [t[:, :64] for t in second]
-    u1 = [dot_full(t, u) for t, u in zip(t1, up1)]
-    m1 = [dot_full(d, turn(t), NT) for t, d in zip(second, down1)]
-    s2 = [s[:64] - dot_full(m[:64], u) for s, m, u in zip(rest, m1, u1)]
-
-    third = run(s2, False)
-    low2 = [s[64:] - dot_full(m[64:], u) for s, m, u in zip(rest, m1, u1)]
-    l0 = first
+        return jnp.where(left, done, 0.0), jnp.where(left, 0.0, done)
+
+    def times(t, half, x):
+        if half:
+            return dot_full(t, jnp.concatenate([jnp.zeros(x.shape, F32), x], axis=0))
+        return dot_full(t[:, :64], x)
+
+    def times_t(x, t, half):
+        return dot_full(x, t, NT) if half else dot_full(x[:, :64], t[:, :64], NT)
+
+    two = range(2)
+    near = [s[:, :128] for s in systems]
+    turned = [turn(x) for x in near]
+    swapped = [turned[0], near[1]]
+    facing = [near[0], turned[1]]
+
+    t0 = run(low, high)
+    u0 = [times(t0[c], c, swapped[c][:64]) for c in two]
+    m0 = [times_t(facing[c][64:128], t0[c], c) for c in two]
+    s1 = [swapped[c][64:128] - dot_full(m0[c], u0[c]) for c in two]
+
+    t1 = run(*s1)
+    v0 = [times(t0[c], c, systems[c][:64, 128:]) for c in two]
+    n0 = [times_t(facing[c][128:], t0[c], c) for c in two]
+    up1 = [systems[c][64:128, 128:] - dot_full(m0[c], v0[c]) for c in two]
+    down1 = [swapped[c][128:] - dot_full(n0[c], u0[c]) for c in two]
+    rest = [systems[c][128:, 128:] - dot_full(n0[c], v0[c]) for c in two]
+    up1, rest = [up1[0], turn(up1[1])], [rest[0], turn(rest[1])]
+    u1 = [times(t1[c], c, up1[c]) for c in two]
+    m1 = [times_t(down1[c], t1[c], c) for c in two]
+    s2 = [rest[c][:64] - dot_full(m1[c][:64], u1[c]) for c in two]
+
+    t2 = run(*s2)
+    low2 = [rest[c][64:] - dot_full(m1[c][64:], u1[c]) for c in two]
+    l0 = [t0[0], turn(t0[1])]
     l1 = [
-        dot_full(t, jnp.where(left, -dot_full(m, p), unit_right))
-        for t, m, p in zip(t1, m0, l0)
+        times(t1[c], c, jnp.where(left, -dot_full(m0[c], l0[c]), unit_right)) for c in two
     ]
-    r2 = [
-        dot_full(n, p) + dot_full(m, q) for n, p, m, q in zip(n0, l0, m1, l1)
-    ]
-    t2 = [t[:, :64] for t in third]
-    u2 = [dot_full(t, s) for t, s in zip(t2, s2)]
-    m2 = [dot_full(s[:, :64], t, NT) for t, s in zip(t2, low2)]
-    s3 = [s - dot_full(m, u) for s, m, u in zip(low2, m2, u2)]
-
-    fourth = run(s3, True)
-    l2 = [-dot_full(t, r[:64]) for t, r in zip(t2, r2)]
-    r3 = [r[64:] + dot_full(m, p) for r, m, p in zip(r2, m2, l2)]
-    r3_right = [jnp.where(left, -dot_full(m, p), unit_right) for m, p in zip(m2, third)]
-    t3 = [t[:, :64] for t in fourth]
+    r2 = [dot_full(n0[c], l0[c]) + dot_full(m1[c], l1[c]) for c in two]
+    u2 = [times(t2[c], c, s2[c]) for c in two]
+    m2 = [times_t(low2[c], t2[c], c) for c in two]
+    s3 = [low2[c] - dot_full(m2[c], u2[c]) for c in two]
+
+    t3 = run(s3[1], s3[0])[::-1]
+    third = [t2[0], turn(t2[1])]
+    l2 = [-times(t2[c], c, r2[c][:64]) for c in two]
+    r3 = [r2[c][64:] + dot_full(m2[c], l2[c]) for c in two]
+    r3_right = [jnp.where(left, -dot_full(m2[c], third[c]), unit_right) for c in two]
     rows = []
-    for c in range(2):
-        last = jnp.concatenate(
-            [-dot_full(t3[c], r3[c]), dot_full(t3[c], r3_right[c])], axis=1
-        )
+    for c in two:
+        last = times(t3[c], 1 - c, jnp.concatenate([-r3[c], r3_right[c]], axis=1))
         rows.append([l0[c], l1[c], jnp.concatenate([l2[c], third[c]], axis=1), last])
     return rows
 
 
-def tapered(refs, falloff, members):
-    grams, forces = [], []
-    for c in range(2):
-        ens, wtd, inn = [], [], []
-        for ref in refs:
-            ensemble = ref[c, :members, :]
-            tail = ref[c, members:, :]
-            weights = tail[1:2, :].astype(F32)
-            ens.append(ensemble)
-            wtd.append((weights * ensemble.astype(F32)).astype(BF16))
-            inn.append(tail)
-        if len(refs) > 1:
-            ens, wtd, inn = (jnp.concatenate(p, axis=1) for p in (ens, wtd, inn))
-        else:
-            ens, wtd, inn = ens[0], wtd[0], inn[0]
-        grams.append(0.5 * falloff * (dot(wtd, ens, NT) + dot(ens, wtd, NT)))
-        forces.append(falloff * dot(inn, wtd, NT)[0:1])
-    grams = [grams[c] + 0.5 * grams[1 - c] for c in range(2)]
-    forces = [forces[c] + 0.5 * forces[1 - c] for c in range(2)]
-    return grams, forces
+def observed_block(refs, c, members):
+    ens, wtd, inn = [], [], []
+    for ref in refs:
+        ensemble = ref[c, :members, :]
+        tail = ref[c, members:, :]
+        weights = tail[1:2, :].astype(F32)
+        ens.append(ensemble)
+        wtd.append((weights * ensemble.astype(F32)).astype(BF16))
+        inn.append(tail)
+    if len(refs) > 1:
+        return tuple(jnp.concatenate(p, axis=1) for p in (ens, wtd, inn))
+    return ens[0], wtd[0], inn[0]
+
+
+def tapered(blocks, falloff, rows, spans):
+    def pick(x):
+        return jnp.concatenate([x[at] for at in spans], axis=0) if len(spans) > 1 else x[spans[0]]
+
+    grams = [
+        0.5 * falloff * (dot(wtd[rows], pick(ens), NT) + dot(ens[rows], pick(wtd), NT))
+        for ens, wtd, _ in blocks
+    ]
+    return [grams[c] + 0.5 * grams[1 - c] for c in range(2)]
+
+
+def tapered_forcing(blocks, falloff):
+    forces = [falloff * dot(inn, wtd, NT)[0:1] for _, wtd, inn in blocks]
+    return [forces[c] + 0.5 * forces[1 - c] for c in range(2)]
 
 
 def gram_kernel(own_ref, system_ref, force_ref, hand_ref):
     members = system_ref.shape[1]
     hand_ref[...] = own_ref[...]
-    grams, forces = tapered([own_ref], 1.0, members)
+    blocks = [observed_block([own_ref], c, members) for c in range(2)]
+    grams = tapered(blocks, 1.0, slice(0, members), [slice(0, members)])
+    forces = tapered_forcing(blocks, 1.0)
     spread = (members - 1) * eye(members, members)
     for c in range(2):
         system_ref[c] = spread + grams[c]
@@ -312,10 +329,17 @@
 def update_kernel(system_ref, force_ref, mate_ref, far_ref, anom_ref, avg_ref, out_ref):
     members = anom_ref.shape[1]
     groups = members // 32
-    grams, forces = tapered([mate_ref, far_ref], 0.5, members)
+    blocks = [observed_block([mate_ref, far_ref], c, members) for c in range(2)]
+    head, whole = slice(0, 64), slice(0, members)
+    low = tapered(blocks, 0.5, head, [slice(0, 128)])[0]
+    high = tapered(blocks, 0.5, head, [slice(64, 128), slice(0, 64)])[1]
+    low = system_ref[0, :64, :128] + low
+    high = pltpu.roll(system_ref[1, :64, :128], 64, 1) + high
+    grams = tapered(blocks, 0.5, whole, [whole])
     systems = [system_ref[c] + grams[c] for c in range(2)]
+    forces = tapered_forcing(blocks, 0.5)
     forces = [force_ref[c] + forces[c] for c in range(2)]
-    inverses = invert256(systems)
+    inverses = invert256(systems, low, high)
     for c in range(2):
         force = forces[c]
         mean_weight = jnp.zeros((1, members), F32)

time: 106 us -> 106 us (level)
  no operation moved by 1% of the time
where the time goes in v4:
time: 106 us
  blocking collectives  37.5 us (35%)
  waiting for transfers between devices  27.8 us (26%)
  starting transfers between devices  25.1 us (24%)
  Pallas kernels  13.2 us (12%)
  local copies, waits for them, and re-layouts  1.91 us (2%)
    all_to_all x1, blocking collectives, on_device(): lax.all_to_all(analyzed.reshape(chunk), TILE_FIRST, split_axis=0, concat_...  37.5 us
    all_to_all x1, waiting for transfers between devices, on_device(): lax.all_to_all(parted, TILE_FIRST, split_axis=0, concat_axis=0, tiled=True)  23.3 us
    all_to_all x1, starting transfers between devices, on_device(): lax.all_to_all(parted, TILE_FIRST, split_axis=0, concat_axis=0, tiled=True)  15.7 us
    pallas_call x1, Pallas kernels, on_device(): call(update_kernel, jax.ShapeDtypeStruct(paired, BF16))  7.44 us
    ppermute x1, starting transfers between devices, on_device(): observed = lax.ppermute(observed, MEM, to_owner)  5.05 us
    ppermute x1, starting transfers between devices, on_device(): far = lax.ppermute(packed, MEM, to_far)  4.32 us
    ppermute x1, waiting for transfers between devices, on_device(): far = lax.ppermute(packed, MEM, to_far)  3.74 us
  transfers between devices with their start and end apart: 4, of which 3 were waited for; matrix products, arithmetic and copies ran while one was open for 0% of the time, Pallas kernels for 1%

profile of v4, /device:TPU:1, one launch (start us, length us, event | category | flops | bytes accessed | tf_op | source)
XLA Modules:
  0.0 105.6 jit_solution(4654968836520243275)
XLA Ops:
  0.0 1.2 %copy-done = bf16[32,8,8,256]{3,2,1,0:T(8,128)(2,1)S(1)} copy-done((bf16[32,8,8,256]{3,2,1,0:T(8,128)(2,1)S(1)}, bf16[32,8,8,256]{3,2,1,0:T(8,128)(2,1)}, u32[]{:S(2)}) %copy-start) | copy-done | bytes 1048600
  1.2 1.7 %shard_map.55 = bf16[256,16,128]{2,1,0:T(8,128)(2,1)} custom-call(bf16[2,1024,256]{2,1,0:T(8,128)(2,1)S(1)} %bitcast.9), custom_call_target="tpu_custom_call" | custom-call | tf_op jit(solution)/shard_map/pallas_call | solution.py:398
  3.0 15.7 %all-to-all-start = ((bf16[256,16,128]{2,1,0:T(8,128)(2,1)}), bf16[256,16,128]{2,1,0:T(8,128)(2,1)S(1)}, u32[]{:S(2)}, u32[]{:S(2)}) async-start(bf16[256,16,128]{2,1,0:T(8,128)(2,1)} %shard_map.55), calls=%async_computation | async-start | bytes 2097152 | tf_op jit(solution)/shard_map/all_to_all | solution.py:410
  18.7 0.0 copy-start.2
  18.7 0.0 copy-start.1
  18.7 0.0 copy-start.3
  18.7 0.0 copy-start.4
  18.7 0.6 copy-done.2
  19.3 0.0 copy-done.1
  19.4 0.0 copy-done.3
  19.4 0.0 copy-done.4
  19.4 0.6 shard_map.56
  19.9 5.1 %collective-permute-start = (f32[8,256]{1,0:T(8,128)S(1)}, f32[8,256]{1,0:T(8,128)S(1)}, u32[]{:S(2)}, u32[]{:S(2)}) collective-permute-start(f32[8,256]{1,0:T(8,128)S(1)} %shard_map.56), channel_id=1, source_target_pairs={{0,0},{1,32},{2,4},{3,36},{4,8},{5,40},{6,12},{7,44},{8,16},{9,48}... | collective-permute-start | bytes 24584 | tf_op jit(solution)/shard_map/ppermute | solution.py:409
  25.0 0.8 collective-permute-done.obs_ref
  25.8 23.3 %all-to-all-done = bf16[256,16,128]{2,1,0:T(8,128)(2,1)S(1)} async-done(((bf16[256,16,128]{2,1,0:T(8,128)(2,1)}), bf16[256,16,128]{2,1,0:T(8,128)(2,1)S(1)}, u32[]{:S(2)}, u32[]{:S(2)}) %all-to-all-start) | async-done | bytes 1048608 | tf_op jit(solution)/shard_map/all_to_all | solution.py:410
  49.1 1.3 %shard_map.57 = (bf16[2,256,1024]{2,1,0:T(8,128)(2,1)S(1)}, f32[2,1,1024]{2,1,0:T(1,128)S(1)}, bf16[2,272,256]{2,1,0:T(8,128)(2,1)S(1)}) custom-call(bf16[16,2,8,16,128]{4,3,2,1,0:T(8,128)(2,1)S(1)} %bitcast.7, f32[8,256]{1,0:T(8,128)S(1)} %collective-permute-done.obs_ref), custom_call_target="tpu_custom_call" | custom-call | tf_op jit(solution)/shard_map/pallas_call | solution.py:411
  50.4 4.3 %collective-permute-start.2 = (bf16[2,272,256]{2,1,0:T(8,128)(2,1)S(1)}, bf16[2,272,256]{2,1,0:T(8,128)(2,1)S(1)}, u32[]{:S(2)}, u32[]{:S(2)}) collective-permute-start(bf16[2,272,256]{2,1,0:T(8,128)(2,1)S(1)} %get-tuple-element.11.own_ref), channel_id=1, source_target_pairs={{32,4},{36,8},{40,12},{44,16},{48,20},{52,24},{56,28},{60,29},{61,... | collective-permute-start | bytes 835592 | tf_op jit(solution)/shard_map/ppermute | solution.py:419
  54.7 0.4 shard_map.58
  55.1 0.1 collective-permute-start.1
  55.2 3.7 %collective-permute-done.2.far_ref = bf16[2,272,256]{2,1,0:T(8,128)(2,1)S(1)} collective-permute-done((bf16[2,272,256]{2,1,0:T(8,128)(2,1)S(1)}, bf16[2,272,256]{2,1,0:T(8,128)(2,1)S(1)}, u32[]{:S(2)}, u32[]{:S(2)}) %collective-permute-start.2) | collective-permute-done | bytes 278560 | tf_op jit(solution)/shard_map/ppermute | solution.py:419
  58.9 0.0 collective-permute-done.1.mate_ref
  58.9 7.4 %shard_map.59 = bf16[16,2,8,16,128]{4,3,2,1,0:T(8,128)(2,1)S(1)} custom-call(f32[2,256,256]{2,1,0:T(8,128)S(1)} %get-tuple-element.12.system_ref, f32[2,1,256]{2,1,0:T(1,128)S(1)} %get-tuple-element.13.force_ref, bf16[2,272,256]{2,1,0:T(8,128)(2,1)S(1)} %collective-permute-done.1.mate_ref, bf16[2,272,256]{2,1,0:T(8,128)(2,1)S(1)} %collective-permute-done.2.far_ref, ...), custom_call_target="tpu_custom_call" | custom-call | tf_op jit(solution)/shard_map/pallas_call | solution.py:429
  66.4 37.5 %all_to_all.10.x_ref = bf16[256,16,128]{2,1,0:T(8,128)(2,1)S(1)} all-to-all(bf16[256,16,128]{2,1,0:T(8,128)(2,1)S(1)} %bitcast.8), channel_id=1, replica_groups=mesh['mem'=8,'tile'=32] {'tile','mem'}, dimensions={0} | all-to-all | bytes 2097152 | tf_op jit(solution)/shard_map/all_to_all | solution.py:433
  103.9 1.8 %shard_map.60 = bf16[2,1024,256]{2,1,0:T(8,128)(2,1)} custom-call(bf16[256,16,128]{2,1,0:T(8,128)(2,1)S(1)} %all_to_all.10.x_ref), custom_call_target="tpu_custom_call" | custom-call | tf_op jit(solution)/shard_map/pallas_call | solution.py:436
  (1 shorter events, 0.0 us)
Async XLA Ops:
  0.0 1.2 %copy-start = (bf16[32,8,8,256]{3,2,1,0:T(8,128)(2,1)S(1)}, bf16[32,8,8,256]{3,2,1,0:T(8,128)(2,1)}, u32[]{:S(2)}) copy-start(bf16[32,8,8,256]{3,2,1,0:T(8,128)(2,1)} %param.5) | copy-start | bytes 3145732
  3.0 46.1 %all-to-all-start = ((bf16[256,16,128]{2,1,0:T(8,128)(2,1)}), bf16[256,16,128]{2,1,0:T(8,128)(2,1)S(1)}, u32[]{:S(2)}, u32[]{:S(2)}) async-start(bf16[256,16,128]{2,1,0:T(8,128)(2,1)} %shard_map.55), calls=%async_computation | async-start | bytes 2097152 | tf_op jit(solution)/shard_map/all_to_all | solution.py:410
  18.7 0.7 copy-start.2
  18.7 0.7 copy-start.1
  18.7 0.7 copy-start.3
  18.7 0.7 copy-start.4
  19.9 5.8 %collective-permute-start = (f32[8,256]{1,0:T(8,128)S(1)}, f32[8,256]{1,0:T(8,128)S(1)}, u32[]{:S(2)}, u32[]{:S(2)}) collective-permute-start(f32[8,256]{1,0:T(8,128)S(1)} %shard_map.56), channel_id=1, source_target_pairs={{0,0},{1,32},{2,4},{3,36},{4,8},{5,40},{6,12},{7,44},{8,16},{9,48}... | collective-permute-start | bytes 24584 | tf_op jit(solution)/shard_map/ppermute | solution.py:409
  50.4 8.5 %collective-permute-start.2 = (bf16[2,272,256]{2,1,0:T(8,128)(2,1)S(1)}, bf16[2,272,256]{2,1,0:T(8,128)(2,1)S(1)}, u32[]{:S(2)}, u32[]{:S(2)}) collective-permute-start(bf16[2,272,256]{2,1,0:T(8,128)(2,1)S(1)} %get-tuple-element.11.own_ref), channel_id=1, source_target_pairs={{32,4},{36,8},{40,12},{44,16},{48,20},{52,24},{56,28},{60,29},{61,... | collective-permute-start | bytes 835592 | tf_op jit(solution)/shard_map/ppermute | solution.py:419
  55.1 3.8 %collective-permute-start.1 = (bf16[2,272,256]{2,1,0:T(8,128)(2,1)S(1)}, bf16[2,272,256]{2,1,0:T(8,128)(2,1)S(1)}, u32[]{:S(2)}, u32[]{:S(2)}) collective-permute-start(bf16[2,272,256]{2,1,0:T(8,128)(2,1)S(1)} %get-tuple-element.14), channel_id=1, source_target_pairs={{0,32},{32,0},{4,36},{36,4},{8,40},{40,8},{12,44},{44,12},{16,48},... | collective-permute-start | bytes 835592 | tf_op jit(solution)/shard_map/ppermute | solution.py:428

commit v5 on v4

--- a/solution.py
+++ b/solution.py
@@ -131,37 +131,22 @@
     return jnp.where(left, low, inner), jnp.where(left, inner, high)
 
 
-def observe_kernel(x_ref, obs_ref, anom_ref, avg_ref, pack_ref):
-    members = anom_ref.shape[1]
-    groups = x_ref.shape[2]
-    cell_total = anom_ref.shape[2]
+def observe_kernel(x_ref, obs_ref, cells_ref, pack_ref):
+    members = cells_ref.shape[1]
+    cell_total = cells_ref.shape[2]
     slots = pack_ref.shape[2]
     for c in range(2):
         for tp in range(8):
-            low = x_ref[c * 8 + tp, 0].astype(F32)
-            high = x_ref[c * 8 + tp, 1].astype(F32)
-            first, second = swap_halves(low, high)
-            cells = jnp.concatenate([first, second], axis=1).reshape(groups * 32, 128)
-            average = jnp.sum(cells, axis=0, keepdims=True) / members
-            anom_ref[c, :, tp * 128 : (tp + 1) * 128] = (cells - average).astype(BF16)
-            avg_ref[c, :, tp * 128 : (tp + 1) * 128] = average
+            first, second = swap_halves(x_ref[c * 8 + tp, 0], x_ref[c * 8 + tp, 1])
+            cells = jnp.concatenate([first, second], axis=1).reshape(members, 128)
+            cells_ref[c, :, tp * 128 : (tp + 1) * 128] = cells
         place = obs_ref[c : c + 1, :].astype(jnp.int32)
         chosen = lax.broadcasted_iota(jnp.int32, (cell_total, slots), 0) == place
         chosen = jnp.where(chosen, 1.0, 0.0).astype(BF16)
-        pack_ref[c, :members, :] = dot(anom_ref[c], chosen).astype(BF16)
-        average = avg_ref[c]
-        top = average.astype(BF16)
-        rest = average - top.astype(F32)
-        middle = rest.astype(BF16)
-        bottom = (rest - middle.astype(F32)).astype(BF16)
-        pieces = jnp.concatenate(
-            [top.astype(F32), middle.astype(F32), bottom.astype(F32)]
-            + [jnp.zeros((13, cell_total), F32)],
-            axis=0,
-        ).astype(BF16)
-        found = dot(pieces, chosen)
-        found = found[0:1] + (found[1:2] + found[2:3])
-        innovation = obs_ref[2 + c : 3 + c, :] - found
+        found = dot(cells_ref[c], chosen)
+        average = jnp.sum(found, axis=0, keepdims=True) / members
+        pack_ref[c, :members, :] = (found - average).astype(BF16)
+        innovation = obs_ref[2 + c : 3 + c, :] - average
         weights = obs_ref[4 + c : 5 + c, :]
         sub = lax.broadcasted_iota(jnp.int32, (16, slots), 0)
         tail = jnp.where(sub == 0, innovation, jnp.where(sub == 1, weights, 0.0))
@@ -324,6 +309,17 @@
     for c in range(2):
         system_ref[c] = spread + grams[c]
         force_ref[c] = forces[c]
+
+
+def anomaly_kernel(cells_ref, force_ref, anom_ref, avg_ref, same_ref):
+    members = cells_ref.shape[1]
+    same_ref[...] = force_ref[...]
+    for c in range(2):
+        for at in range(0, cells_ref.shape[2], 128):
+            cells = cells_ref[c, :, at : at + 128].astype(F32)
+            average = jnp.sum(cells, axis=0, keepdims=True) / members
+            anom_ref[c, :, at : at + 128] = (cells - average).astype(BF16)
+            avg_ref[c, :, at : at + 128] = average
 
 
 def update_kernel(system_ref, force_ref, mate_ref, far_ref, anom_ref, avg_ref, out_ref):
@@ -408,11 +404,10 @@
     )(measured_position[0], measured_datum[0], measured_noise_spread[0], measured_tally)
     observed = lax.ppermute(observed, MEM, to_owner)
     relaid = lax.all_to_all(parted, TILE_FIRST, split_axis=0, concat_axis=0, tiled=True)
-    anomaly, average, packed = call(
+    row_cells, packed = call(
         observe_kernel,
         (
             jax.ShapeDtypeStruct((2, members, cells), BF16),
-            jax.ShapeDtypeStruct((2, 1, cells), F32),
             jax.ShapeDtypeStruct((2, members + 16, slots), BF16),
         ),
     )(relaid.reshape(paired), observed)
@@ -426,6 +421,14 @@
         ),
     )(packed)
     mate = lax.ppermute(hand, MEM, to_mate)
+    anomaly, average, force = call(
+        anomaly_kernel,
+        (
+            jax.ShapeDtypeStruct((2, members, cells), BF16),
+            jax.ShapeDtypeStruct((2, 1, cells), F32),
+            jax.ShapeDtypeStruct(force.shape, F32),
+        ),
+    )(row_cells, force)
     analyzed = call(
         update_kernel,
         jax.ShapeDtypeStruct(paired, BF16),

time: 106 us -> 105 us (level)
  no operation moved by 1% of the time
where the time goes in v5:
time: 105 us
  blocking collectives  37.5 us (36%)
  waiting for transfers between devices  27.4 us (26%)
  starting transfers between devices  25.1 us (24%)
  Pallas kernels  13.1 us (12%)
  local copies, waits for them, and re-layouts  1.91 us (2%)
    all_to_all x1, blocking collectives, on_device(): lax.all_to_all(analyzed.reshape(chunk), TILE_FIRST, split_axis=0, concat_...  37.5 us
    all_to_all x1, waiting for transfers between devices, on_device(): lax.all_to_all(parted, TILE_FIRST, split_axis=0, concat_axis=0, tiled=True)  23.3 us
    all_to_all x1, starting transfers between devices, on_device(): lax.all_to_all(parted, TILE_FIRST, split_axis=0, concat_axis=0, tiled=True)  15.7 us
    pallas_call x1, Pallas kernels, on_device(): call(update_kernel, jax.ShapeDtypeStruct(paired, BF16))  7.44 us
    ppermute x1, starting transfers between devices, on_device(): observed = lax.ppermute(observed, MEM, to_owner)  5.05 us
    ppermute x1, starting transfers between devices, on_device(): far = lax.ppermute(packed, MEM, to_far)  4.32 us
    ppermute x1, waiting for transfers between devices, on_device(): far = lax.ppermute(packed, MEM, to_far)  3.25 us
  transfers between devices with their start and end apart: 4, of which 3 were waited for; matrix products, arithmetic and copies ran while one was open for 0% of the time, Pallas kernels for 1%

profile of v5, /device:TPU:1, one launch (start us, length us, event | category | flops | bytes accessed | tf_op | source)
XLA Modules:
  0.0 105.0 jit_solution(9885838817723379471)
XLA Ops:
  0.0 1.2 %copy-done = bf16[32,8,8,256]{3,2,1,0:T(8,128)(2,1)S(1)} copy-done((bf16[32,8,8,256]{3,2,1,0:T(8,128)(2,1)S(1)}, bf16[32,8,8,256]{3,2,1,0:T(8,128)(2,1)}, u32[]{:S(2)}) %copy-start) | copy-done | bytes 1048600
  1.2 1.7 %shard_map.55 = bf16[256,16,128]{2,1,0:T(8,128)(2,1)} custom-call(bf16[2,1024,256]{2,1,0:T(8,128)(2,1)S(1)} %bitcast.9), custom_call_target="tpu_custom_call" | custom-call | tf_op jit(solution)/shard_map/pallas_call | solution.py:394
  3.0 15.7 %all-to-all-start = ((bf16[256,16,128]{2,1,0:T(8,128)(2,1)}), bf16[256,16,128]{2,1,0:T(8,128)(2,1)S(1)}, u32[]{:S(2)}, u32[]{:S(2)}) async-start(bf16[256,16,128]{2,1,0:T(8,128)(2,1)} %shard_map.55), calls=%async_computation | async-start | bytes 2097152 | tf_op jit(solution)/shard_map/all_to_all | solution.py:406
  18.7 0.0 copy-start.2
  18.7 0.0 copy-start.1
  18.7 0.0 copy-start.3
  18.7 0.0 copy-start.4
  18.7 0.6 copy-done.2
  19.3 0.0 copy-done.1
  19.4 0.0 copy-done.3
  19.4 0.6 shard_map.56
  19.9 5.1 %collective-permute-start = (f32[8,256]{1,0:T(8,128)S(1)}, f32[8,256]{1,0:T(8,128)S(1)}, u32[]{:S(2)}, u32[]{:S(2)}) collective-permute-start(f32[8,256]{1,0:T(8,128)S(1)} %shard_map.56), channel_id=1, source_target_pairs={{0,0},{1,32},{2,4},{3,36},{4,8},{5,40},{6,12},{7,44},{8,16},{9,48}... | collective-permute-start | bytes 24584 | tf_op jit(solution)/shard_map/ppermute | solution.py:405
  25.0 0.8 collective-permute-done.obs_ref
  25.8 23.3 %all-to-all-done = bf16[256,16,128]{2,1,0:T(8,128)(2,1)S(1)} async-done(((bf16[256,16,128]{2,1,0:T(8,128)(2,1)}), bf16[256,16,128]{2,1,0:T(8,128)(2,1)S(1)}, u32[]{:S(2)}, u32[]{:S(2)}) %all-to-all-start) | async-done | bytes 1048608 | tf_op jit(solution)/shard_map/all_to_all | solution.py:406
  49.1 0.7 shard_map.57
  49.8 4.3 %collective-permute-start.2 = (bf16[2,272,256]{2,1,0:T(8,128)(2,1)S(1)}, bf16[2,272,256]{2,1,0:T(8,128)(2,1)S(1)}, u32[]{:S(2)}, u32[]{:S(2)}) collective-permute-start(bf16[2,272,256]{2,1,0:T(8,128)(2,1)S(1)} %get-tuple-element.13.own_ref), channel_id=1, source_target_pairs={{32,4},{36,8},{40,12},{44,16},{48,20},{52,24},{56,28},{60,29},{61,... | collective-permute-start | bytes 835592 | tf_op jit(solution)/shard_map/ppermute | solution.py:414
  54.1 0.4 shard_map.58
  54.5 0.1 collective-permute-start.1
  54.6 0.5 shard_map.59
  55.1 3.2 %collective-permute-done.2.far_ref = bf16[2,272,256]{2,1,0:T(8,128)(2,1)S(1)} collective-permute-done((bf16[2,272,256]{2,1,0:T(8,128)(2,1)S(1)}, bf16[2,272,256]{2,1,0:T(8,128)(2,1)S(1)}, u32[]{:S(2)}, u32[]{:S(2)}) %collective-permute-start.2) | collective-permute-done | bytes 278560 | tf_op jit(solution)/shard_map/ppermute | solution.py:414
  58.4 0.0 collective-permute-done.1.mate_ref
  58.4 7.4 %shard_map.60 = bf16[16,2,8,16,128]{4,3,2,1,0:T(8,128)(2,1)S(1)} custom-call(f32[2,256,256]{2,1,0:T(8,128)S(1)} %get-tuple-element.14.system_ref, f32[2,1,256]{2,1,0:T(1,128)S(1)} %get-tuple-element.17.force_ref, bf16[2,272,256]{2,1,0:T(8,128)(2,1)S(1)} %collective-permute-done.1.mate_ref, bf16[2,272,256]{2,1,0:T(8,128)(2,1)S(1)} %collective-permute-done.2.far_ref, ...), custom_call_target="tpu_custom_call" | custom-call | tf_op jit(solution)/shard_map/pallas_call | solution.py:432
  65.8 37.5 %all_to_all.10.x_ref = bf16[256,16,128]{2,1,0:T(8,128)(2,1)S(1)} all-to-all(bf16[256,16,128]{2,1,0:T(8,128)(2,1)S(1)} %bitcast.8), channel_id=1, replica_groups=mesh['mem'=8,'tile'=32] {'tile','mem'}, dimensions={0} | all-to-all | bytes 2097152 | tf_op jit(solution)/shard_map/all_to_all | solution.py:436
  103.3 1.8 %shard_map.61 = bf16[2,1024,256]{2,1,0:T(8,128)(2,1)} custom-call(bf16[256,16,128]{2,1,0:T(8,128)(2,1)S(1)} %all_to_all.10.x_ref), custom_call_target="tpu_custom_call" | custom-call | tf_op jit(solution)/shard_map/pallas_call | solution.py:439
  (2 shorter events, 0.0 us)
Async XLA Ops:
  0.0 1.2 %copy-start = (bf16[32,8,8,256]{3,2,1,0:T(8,128)(2,1)S(1)}, bf16[32,8,8,256]{3,2,1,0:T(8,128)(2,1)}, u32[]{:S(2)}) copy-start(bf16[32,8,8,256]{3,2,1,0:T(8,128)(2,1)} %param.5) | copy-start | bytes 3145732
  3.0 46.1 %all-to-all-start = ((bf16[256,16,128]{2,1,0:T(8,128)(2,1)}), bf16[256,16,128]{2,1,0:T(8,128)(2,1)S(1)}, u32[]{:S(2)}, u32[]{:S(2)}) async-start(bf16[256,16,128]{2,1,0:T(8,128)(2,1)} %shard_map.55), calls=%async_computation | async-start | bytes 2097152 | tf_op jit(solution)/shard_map/all_to_all | solution.py:406
  18.7 0.7 copy-start.2
  18.7 0.7 copy-start.1
  18.7 0.7 copy-start.3
  18.7 0.7 copy-start.4
  19.9 5.8 %collective-permute-start = (f32[8,256]{1,0:T(8,128)S(1)}, f32[8,256]{1,0:T(8,128)S(1)}, u32[]{:S(2)}, u32[]{:S(2)}) collective-permute-start(f32[8,256]{1,0:T(8,128)S(1)} %shard_map.56), channel_id=1, source_target_pairs={{0,0},{1,32},{2,4},{3,36},{4,8},{5,40},{6,12},{7,44},{8,16},{9,48}... | collective-permute-start | bytes 24584 | tf_op jit(solution)/shard_map/ppermute | solution.py:405
  49.8 8.5 %collective-permute-start.2 = (bf16[2,272,256]{2,1,0:T(8,128)(2,1)S(1)}, bf16[2,272,256]{2,1,0:T(8,128)(2,1)S(1)}, u32[]{:S(2)}, u32[]{:S(2)}) collective-permute-start(bf16[2,272,256]{2,1,0:T(8,128)(2,1)S(1)} %get-tuple-element.13.own_ref), channel_id=1, source_target_pairs={{32,4},{36,8},{40,12},{44,16},{48,20},{52,24},{56,28},{60,29},{61,... | collective-permute-start | bytes 835592 | tf_op jit(solution)/shard_map/ppermute | solution.py:414
  54.5 3.8 %collective-permute-start.1 = (bf16[2,272,256]{2,1,0:T(8,128)(2,1)S(1)}, bf16[2,272,256]{2,1,0:T(8,128)(2,1)S(1)}, u32[]{:S(2)}, u32[]{:S(2)}) collective-permute-start(bf16[2,272,256]{2,1,0:T(8,128)(2,1)S(1)} %get-tuple-element.18), channel_id=1, source_target_pairs={{0,32},{32,0},{4,36},{36,4},{8,40},{40,8},{12,44},{44,12},{16,48},... | collective-permute-start | bytes 835592 | tf_op jit(solution)/shard_map/ppermute | solution.py:423

commit v6 on v5

--- a/solution.py
+++ b/solution.py
@@ -378,7 +378,7 @@
     half = part * level_count * width // 2
     scratch = [
         pltpu.VMEM((PIECES, 2, half // PIECES, line_total), BF16),
-        pltpu.VMEM((line_total * 16, 128), F32),
+        pltpu.VMEM((line_total * 16 + 128, 128), F32),
         pltpu.SemaphoreType.DMA((PIECES,)),
     ]
     places = np.arange(line_total)

time: 105 us -> 105 us (level)
  no operation moved by 1% of the time
where the time goes in v6:
time: 105 us
  blocking collectives  37.5 us (36%)
  waiting for transfers between devices  27.4 us (26%)
  starting transfers between devices  25.1 us (24%)
  Pallas kernels  13.1 us (12%)
  local copies, waits for them, and re-layouts  1.91 us (2%)
    all_to_all x1, blocking collectives, on_device(): lax.all_to_all(analyzed.reshape(chunk), TILE_FIRST, split_axis=0, concat_...  37.5 us
    all_to_all x1, waiting for transfers between devices, on_device(): lax.all_to_all(parted, TILE_FIRST, split_axis=0, concat_axis=0, tiled=True)  23.3 us
    all_to_all x1, starting transfers between devices, on_device(): lax.all_to_all(parted, TILE_FIRST, split_axis=0, concat_axis=0, tiled=True)  15.7 us
    pallas_call x1, Pallas kernels, on_device(): call(update_kernel, jax.ShapeDtypeStruct(paired, BF16))  7.44 us
    ppermute x1, starting transfers between devices, on_device(): observed = lax.ppermute(observed, MEM, to_owner)  5.05 us
    ppermute x1, starting transfers between devices, on_device(): far = lax.ppermute(packed, MEM, to_far)  4.32 us
    ppermute x1, waiting for transfers between devices, on_device(): far = lax.ppermute(packed, MEM, to_far)  3.25 us
  transfers between devices with their start and end apart: 4, of which 3 were waited for; matrix products, arithmetic and copies ran while one was open for 0% of the time, Pallas kernels for 1%

profile of v6, /device:TPU:1, one launch (start us, length us, event | category | flops | bytes accessed | tf_op | source)
XLA Modules:
  0.0 105.0 jit_solution(1222047290353549539)
XLA Ops:
  0.0 1.2 %copy-done = bf16[32,8,8,256]{3,2,1,0:T(8,128)(2,1)S(1)} copy-done((bf16[32,8,8,256]{3,2,1,0:T(8,128)(2,1)S(1)}, bf16[32,8,8,256]{3,2,1,0:T(8,128)(2,1)}, u32[]{:S(2)}) %copy-start) | copy-done | bytes 1048600
  1.2 1.7 %shard_map.55 = bf16[256,16,128]{2,1,0:T(8,128)(2,1)} custom-call(bf16[2,1024,256]{2,1,0:T(8,128)(2,1)S(1)} %bitcast.9), custom_call_target="tpu_custom_call" | custom-call | tf_op jit(solution)/shard_map/pallas_call | solution.py:394
  3.0 15.7 %all-to-all-start = ((bf16[256,16,128]{2,1,0:T(8,128)(2,1)}), bf16[256,16,128]{2,1,0:T(8,128)(2,1)S(1)}, u32[]{:S(2)}, u32[]{:S(2)}) async-start(bf16[256,16,128]{2,1,0:T(8,128)(2,1)} %shard_map.55), calls=%async_computation | async-start | bytes 2097152 | tf_op jit(solution)/shard_map/all_to_all | solution.py:406
  18.7 0.0 copy-start.2
  18.7 0.0 copy-start.1
  18.7 0.0 copy-start.3
  18.7 0.0 copy-start.4
  18.7 0.6 copy-done.2
  19.3 0.0 copy-done.1
  19.4 0.0 copy-done.3
  19.4 0.6 shard_map.56
  19.9 5.1 %collective-permute-start = (f32[8,256]{1,0:T(8,128)S(1)}, f32[8,256]{1,0:T(8,128)S(1)}, u32[]{:S(2)}, u32[]{:S(2)}) collective-permute-start(f32[8,256]{1,0:T(8,128)S(1)} %shard_map.56), channel_id=1, source_target_pairs={{0,0},{1,32},{2,4},{3,36},{4,8},{5,40},{6,12},{7,44},{8,16},{9,48}... | collective-permute-start | bytes 24584 | tf_op jit(solution)/shard_map/ppermute | solution.py:405
  25.0 0.8 collective-permute-done.obs_ref
  25.8 23.3 %all-to-all-done = bf16[256,16,128]{2,1,0:T(8,128)(2,1)S(1)} async-done(((bf16[256,16,128]{2,1,0:T(8,128)(2,1)}), bf16[256,16,128]{2,1,0:T(8,128)(2,1)S(1)}, u32[]{:S(2)}, u32[]{:S(2)}) %all-to-all-start) | async-done | bytes 1048608 | tf_op jit(solution)/shard_map/all_to_all | solution.py:406
  49.1 0.7 shard_map.57
  49.8 4.3 %collective-permute-start.2 = (bf16[2,272,256]{2,1,0:T(8,128)(2,1)S(1)}, bf16[2,272,256]{2,1,0:T(8,128)(2,1)S(1)}, u32[]{:S(2)}, u32[]{:S(2)}) collective-permute-start(bf16[2,272,256]{2,1,0:T(8,128)(2,1)S(1)} %get-tuple-element.13.own_ref), channel_id=1, source_target_pairs={{32,4},{36,8},{40,12},{44,16},{48,20},{52,24},{56,28},{60,29},{61,... | collective-permute-start | bytes 835592 | tf_op jit(solution)/shard_map/ppermute | solution.py:414
  54.1 0.4 shard_map.58
  54.5 0.1 collective-permute-start.1
  54.6 0.5 shard_map.59
  55.1 3.2 %collective-permute-done.2.far_ref = bf16[2,272,256]{2,1,0:T(8,128)(2,1)S(1)} collective-permute-done((bf16[2,272,256]{2,1,0:T(8,128)(2,1)S(1)}, bf16[2,272,256]{2,1,0:T(8,128)(2,1)S(1)}, u32[]{:S(2)}, u32[]{:S(2)}) %collective-permute-start.2) | collective-permute-done | bytes 278560 | tf_op jit(solution)/shard_map/ppermute | solution.py:414
  58.4 0.0 collective-permute-done.1.mate_ref
  58.4 7.4 %shard_map.60 = bf16[16,2,8,16,128]{4,3,2,1,0:T(8,128)(2,1)S(1)} custom-call(f32[2,256,256]{2,1,0:T(8,128)S(1)} %get-tuple-element.14.system_ref, f32[2,1,256]{2,1,0:T(1,128)S(1)} %get-tuple-element.17.force_ref, bf16[2,272,256]{2,1,0:T(8,128)(2,1)S(1)} %collective-permute-done.1.mate_ref, bf16[2,272,256]{2,1,0:T(8,128)(2,1)S(1)} %collective-permute-done.2.far_ref, ...), custom_call_target="tpu_custom_call" | custom-call | tf_op jit(solution)/shard_map/pallas_call | solution.py:432
  65.8 37.5 %all_to_all.10.x_ref = bf16[256,16,128]{2,1,0:T(8,128)(2,1)S(1)} all-to-all(bf16[256,16,128]{2,1,0:T(8,128)(2,1)S(1)} %bitcast.8), channel_id=1, replica_groups=mesh['mem'=8,'tile'=32] {'tile','mem'}, dimensions={0} | all-to-all | bytes 2097152 | tf_op jit(solution)/shard_map/all_to_all | solution.py:436
  103.3 1.8 %shard_map.61 = bf16[2,1024,256]{2,1,0:T(8,128)(2,1)} custom-call(bf16[256,16,128]{2,1,0:T(8,128)(2,1)S(1)} %all_to_all.10.x_ref), custom_call_target="tpu_custom_call" | custom-call | tf_op jit(solution)/shard_map/pallas_call | solution.py:439
  (2 shorter events, 0.0 us)
Async XLA Ops:
  0.0 1.2 %copy-start = (bf16[32,8,8,256]{3,2,1,0:T(8,128)(2,1)S(1)}, bf16[32,8,8,256]{3,2,1,0:T(8,128)(2,1)}, u32[]{:S(2)}) copy-start(bf16[32,8,8,256]{3,2,1,0:T(8,128)(2,1)} %param.5) | copy-start | bytes 3145732
  3.0 46.1 %all-to-all-start = ((bf16[256,16,128]{2,1,0:T(8,128)(2,1)}), bf16[256,16,128]{2,1,0:T(8,128)(2,1)S(1)}, u32[]{:S(2)}, u32[]{:S(2)}) async-start(bf16[256,16,128]{2,1,0:T(8,128)(2,1)} %shard_map.55), calls=%async_computation | async-start | bytes 2097152 | tf_op jit(solution)/shard_map/all_to_all | solution.py:406
  18.7 0.7 copy-start.2
  18.7 0.7 copy-start.1
  18.7 0.7 copy-start.3
  18.7 0.7 copy-start.4
  19.9 5.8 %collective-permute-start = (f32[8,256]{1,0:T(8,128)S(1)}, f32[8,256]{1,0:T(8,128)S(1)}, u32[]{:S(2)}, u32[]{:S(2)}) collective-permute-start(f32[8,256]{1,0:T(8,128)S(1)} %shard_map.56), channel_id=1, source_target_pairs={{0,0},{1,32},{2,4},{3,36},{4,8},{5,40},{6,12},{7,44},{8,16},{9,48}... | collective-permute-start | bytes 24584 | tf_op jit(solution)/shard_map/ppermute | solution.py:405
  49.8 8.5 %collective-permute-start.2 = (bf16[2,272,256]{2,1,0:T(8,128)(2,1)S(1)}, bf16[2,272,256]{2,1,0:T(8,128)(2,1)S(1)}, u32[]{:S(2)}, u32[]{:S(2)}) collective-permute-start(bf16[2,272,256]{2,1,0:T(8,128)(2,1)S(1)} %get-tuple-element.13.own_ref), channel_id=1, source_target_pairs={{32,4},{36,8},{40,12},{44,16},{48,20},{52,24},{56,28},{60,29},{61,... | collective-permute-start | bytes 835592 | tf_op jit(solution)/shard_map/ppermute | solution.py:414
  54.5 3.8 %collective-permute-start.1 = (bf16[2,272,256]{2,1,0:T(8,128)(2,1)S(1)}, bf16[2,272,256]{2,1,0:T(8,128)(2,1)S(1)}, u32[]{:S(2)}, u32[]{:S(2)}) collective-permute-start(bf16[2,272,256]{2,1,0:T(8,128)(2,1)S(1)} %get-tuple-element.18), channel_id=1, source_target_pairs={{0,32},{32,0},{4,36},{36,4},{8,40},{40,8},{12,44},{44,12},{16,48},... | collective-permute-start | bytes 835592 | tf_op jit(solution)/shard_map/ppermute | solution.py:423

commit v7 on v6

--- a/solution.py
+++ b/solution.py
@@ -50,9 +50,9 @@
 
 def row_of(tile, mem):
     x, core, z, y = mem >> 1, mem & 1, tile >> 2, tile & 3
-    along_y = y + (x & 1) * (3 - 2 * y)
-    along_z = z + (along_y & 1) * (7 - 2 * z)
-    return 2 * (x * 32 + along_y * 8 + along_z) + core
+    along_y = y + (z & 1) * (3 - 2 * y)
+    along_x = x + (along_y & 1) * (3 - 2 * x)
+    return 2 * (z * 16 + along_y * 4 + along_x) + core
 
 
 def row_of_chunk(chunk):

time: 105 us -> 104 us (level)
    all_to_all x1, waiting for transfers between devices: 23.3 us -> 16.9 us  [on_device(): lax.all_to_all(parted, TILE_FIRST, split_axis=0, concat_axis=0, tiled=True)]
    ppermute x1, waiting for transfers between devices: 0.77 us -> 6.26 us  [on_device(): observed = lax.ppermute(observed, MEM, to_owner)]
where the time goes in v7:
time: 104 us
  blocking collectives  37 us (36%)
  waiting for transfers between devices  26.4 us (25%)
  starting transfers between devices  25.7 us (25%)
  Pallas kernels  13 us (12%)
  local copies, waits for them, and re-layouts  1.91 us (2%)
    all_to_all x1, blocking collectives, on_device(): lax.all_to_all(analyzed.reshape(chunk), TILE_FIRST, split_axis=0, concat_...  37 us
    all_to_all x1, waiting for transfers between devices, on_device(): lax.all_to_all(parted, TILE_FIRST, split_axis=0, concat_axis=0, tiled=True)  16.9 us
    all_to_all x1, starting transfers between devices, on_device(): lax.all_to_all(parted, TILE_FIRST, split_axis=0, concat_axis=0, tiled=True)  15.7 us
    pallas_call x1, Pallas kernels, on_device(): call(update_kernel, jax.ShapeDtypeStruct(paired, BF16))  7.44 us
    ppermute x1, waiting for transfers between devices, on_device(): observed = lax.ppermute(observed, MEM, to_owner)  6.26 us
    ppermute x1, starting transfers between devices, on_device(): observed = lax.ppermute(observed, MEM, to_owner)  5.97 us
    ppermute x1, starting transfers between devices, on_device(): far = lax.ppermute(packed, MEM, to_far)  3.94 us
    ppermute x1, waiting for transfers between devices, on_device(): far = lax.ppermute(packed, MEM, to_far)  3.25 us
  transfers between devices with their start and end apart: 4, of which 3 were waited for; matrix products, arithmetic and copies ran while one was open for 0% of the time, Pallas kernels for 1%

profile of v7, /device:TPU:1, one launch (start us, length us, event | category | flops | bytes accessed | tf_op | source)
XLA Modules:
  0.0 104.1 jit_solution(18370641460520014665)
XLA Ops:
  0.0 1.2 %copy-done = bf16[32,8,8,256]{3,2,1,0:T(8,128)(2,1)S(1)} copy-done((bf16[32,8,8,256]{3,2,1,0:T(8,128)(2,1)S(1)}, bf16[32,8,8,256]{3,2,1,0:T(8,128)(2,1)}, u32[]{:S(2)}) %copy-start) | copy-done | bytes 1048600
  1.2 1.7 %shard_map.55 = bf16[256,16,128]{2,1,0:T(8,128)(2,1)} custom-call(bf16[2,1024,256]{2,1,0:T(8,128)(2,1)S(1)} %bitcast.9), custom_call_target="tpu_custom_call" | custom-call | tf_op jit(solution)/shard_map/pallas_call | solution.py:394
  3.0 15.7 %all-to-all-start = ((bf16[256,16,128]{2,1,0:T(8,128)(2,1)}), bf16[256,16,128]{2,1,0:T(8,128)(2,1)S(1)}, u32[]{:S(2)}, u32[]{:S(2)}) async-start(bf16[256,16,128]{2,1,0:T(8,128)(2,1)} %shard_map.55), calls=%async_computation | async-start | bytes 2097152 | tf_op jit(solution)/shard_map/all_to_all | solution.py:406
  18.7 0.0 copy-start.2
  18.7 0.0 copy-start.1
  18.7 0.0 copy-start.3
  18.7 0.0 copy-start.4
  18.7 0.6 copy-done.2
  19.3 0.0 copy-done.1
  19.4 0.0 copy-done.3
  19.4 0.6 shard_map.56
  19.9 6.0 %collective-permute-start = (f32[8,256]{1,0:T(8,128)S(1)}, f32[8,256]{1,0:T(8,128)S(1)}, u32[]{:S(2)}, u32[]{:S(2)}) collective-permute-start(f32[8,256]{1,0:T(8,128)S(1)} %shard_map.56), channel_id=1, source_target_pairs={{0,0},{1,32},{2,64},{3,96},{4,128},{5,160},{6,192},{7,224},{8,193}... | collective-permute-start | bytes 24584 | tf_op jit(solution)/shard_map/ppermute | solution.py:405
  25.9 6.3 %collective-permute-done.obs_ref = f32[8,256]{1,0:T(8,128)S(1)} collective-permute-done((f32[8,256]{1,0:T(8,128)S(1)}, f32[8,256]{1,0:T(8,128)S(1)}, u32[]{:S(2)}, u32[]{:S(2)}) %collective-permute-start) | collective-permute-done | bytes 8224 | tf_op jit(solution)/shard_map/ppermute | solution.py:405
  32.2 16.9 %all-to-all-done = bf16[256,16,128]{2,1,0:T(8,128)(2,1)S(1)} async-done(((bf16[256,16,128]{2,1,0:T(8,128)(2,1)}), bf16[256,16,128]{2,1,0:T(8,128)(2,1)S(1)}, u32[]{:S(2)}, u32[]{:S(2)}) %all-to-all-start) | async-done | bytes 1048608 | tf_op jit(solution)/shard_map/all_to_all | solution.py:406
  49.0 0.7 shard_map.57
  49.7 3.9 %collective-permute-start.2 = (bf16[2,272,256]{2,1,0:T(8,128)(2,1)S(1)}, bf16[2,272,256]{2,1,0:T(8,128)(2,1)S(1)}, u32[]{:S(2)}, u32[]{:S(2)}) collective-permute-start(bf16[2,272,256]{2,1,0:T(8,128)(2,1)S(1)} %get-tuple-element.13.own_ref), channel_id=1, source_target_pairs={{32,64},{96,128},{160,192},{224,193},{225,129},{161,65},{97,1},{33... | collective-permute-start | bytes 835592 | tf_op jit(solution)/shard_map/ppermute | solution.py:414
  53.7 0.4 shard_map.58
  54.1 0.1 collective-permute-start.1
  54.2 0.5 shard_map.59
  54.7 3.2 %collective-permute-done.2.far_ref = bf16[2,272,256]{2,1,0:T(8,128)(2,1)S(1)} collective-permute-done((bf16[2,272,256]{2,1,0:T(8,128)(2,1)S(1)}, bf16[2,272,256]{2,1,0:T(8,128)(2,1)S(1)}, u32[]{:S(2)}, u32[]{:S(2)}) %collective-permute-start.2) | collective-permute-done | bytes 278560 | tf_op jit(solution)/shard_map/ppermute | solution.py:414
  57.9 0.0 collective-permute-done.1.mate_ref
  57.9 7.4 %shard_map.60 = bf16[16,2,8,16,128]{4,3,2,1,0:T(8,128)(2,1)S(1)} custom-call(f32[2,256,256]{2,1,0:T(8,128)S(1)} %get-tuple-element.14.system_ref, f32[2,1,256]{2,1,0:T(1,128)S(1)} %get-tuple-element.17.force_ref, bf16[2,272,256]{2,1,0:T(8,128)(2,1)S(1)} %collective-permute-done.1.mate_ref, bf16[2,272,256]{2,1,0:T(8,128)(2,1)S(1)} %collective-permute-done.2.far_ref, ...), custom_call_target="tpu_custom_call" | custom-call | tf_op jit(solution)/shard_map/pallas_call | solution.py:432
  65.4 37.0 %all_to_all.10.x_ref = bf16[256,16,128]{2,1,0:T(8,128)(2,1)S(1)} all-to-all(bf16[256,16,128]{2,1,0:T(8,128)(2,1)S(1)} %bitcast.8), channel_id=1, replica_groups=mesh['mem'=8,'tile'=32] {'tile','mem'}, dimensions={0} | all-to-all | bytes 2097152 | tf_op jit(solution)/shard_map/all_to_all | solution.py:436
  102.4 1.7 %shard_map.61 = bf16[2,1024,256]{2,1,0:T(8,128)(2,1)} custom-call(bf16[256,16,128]{2,1,0:T(8,128)(2,1)S(1)} %all_to_all.10.x_ref), custom_call_target="tpu_custom_call" | custom-call | tf_op jit(solution)/shard_map/pallas_call | solution.py:439
  (2 shorter events, 0.0 us)
Async XLA Ops:
  0.0 1.2 %copy-start = (bf16[32,8,8,256]{3,2,1,0:T(8,128)(2,1)S(1)}, bf16[32,8,8,256]{3,2,1,0:T(8,128)(2,1)}, u32[]{:S(2)}) copy-start(bf16[32,8,8,256]{3,2,1,0:T(8,128)(2,1)} %param.5) | copy-start | bytes 3145732
  3.0 46.0 %all-to-all-start = ((bf16[256,16,128]{2,1,0:T(8,128)(2,1)}), bf16[256,16,128]{2,1,0:T(8,128)(2,1)S(1)}, u32[]{:S(2)}, u32[]{:S(2)}) async-start(bf16[256,16,128]{2,1,0:T(8,128)(2,1)} %shard_map.55), calls=%async_computation | async-start | bytes 2097152 | tf_op jit(solution)/shard_map/all_to_all | solution.py:406
  18.7 0.7 copy-start.2
  18.7 0.7 copy-start.1
  18.7 0.7 copy-start.3
  18.7 0.7 copy-start.4
  19.9 12.2 %collective-permute-start = (f32[8,256]{1,0:T(8,128)S(1)}, f32[8,256]{1,0:T(8,128)S(1)}, u32[]{:S(2)}, u32[]{:S(2)}) collective-permute-start(f32[8,256]{1,0:T(8,128)S(1)} %shard_map.56), channel_id=1, source_target_pairs={{0,0},{1,32},{2,64},{3,96},{4,128},{5,160},{6,192},{7,224},{8,193}... | collective-permute-start | bytes 24584 | tf_op jit(solution)/shard_map/ppermute | solution.py:405
  49.7 8.2 %collective-permute-start.2 = (bf16[2,272,256]{2,1,0:T(8,128)(2,1)S(1)}, bf16[2,272,256]{2,1,0:T(8,128)(2,1)S(1)}, u32[]{:S(2)}, u32[]{:S(2)}) collective-permute-start(bf16[2,272,256]{2,1,0:T(8,128)(2,1)S(1)} %get-tuple-element.13.own_ref), channel_id=1, source_target_pairs={{32,64},{96,128},{160,192},{224,193},{225,129},{161,65},{97,1},{33... | collective-permute-start | bytes 835592 | tf_op jit(solution)/shard_map/ppermute | solution.py:414
  54.1 3.8 %collective-permute-start.1 = (bf16[2,272,256]{2,1,0:T(8,128)(2,1)S(1)}, bf16[2,272,256]{2,1,0:T(8,128)(2,1)S(1)}, u32[]{:S(2)}, u32[]{:S(2)}) collective-permute-start(bf16[2,272,256]{2,1,0:T(8,128)(2,1)S(1)} %get-tuple-element.18), channel_id=1, source_target_pairs={{0,32},{32,0},{64,96},{96,64},{128,160},{160,128},{192,224},{224,1... | collective-permute-start | bytes 835592 | tf_op jit(solution)/shard_map/ppermute | solution.py:423
